TPU v7x, 32 devices: a whole 2x2x4 slice. The times are simulated.
32 devices in a mesh: ba: 8 (over z, x), pb: 4 (over y, core).
Axes of the slice: x: 2, y: 2, z: 4, core: 2. Of those that a mesh axis runs over, the one named last changes fastest.
Arguments:
- decoder_input: bfloat16 [64, 100, 512], P('ba', 'pb'), may hold values from -6 to 6
- memory: bfloat16 [64, 1208, 512], P('ba'), may hold values from -6 to 6
- lengths: int32 [64], P('ba'), may hold values from 302 to 1208, as said below
- query_embed: bfloat16 [100, 512], P('pb'), may hold values from -6 to 6
- self_query: bfloat16 [512, 512], replicated, may hold values from -0.25 to 0.25
- self_query_bias: bfloat16 [512], replicated, may hold values from -2 to 2
- self_key: bfloat16 [512, 512], replicated, may hold values from -0.25 to 0.25
- self_value: bfloat16 [512, 512], replicated, may hold values from -0.25 to 0.25
- self_value_bias: bfloat16 [512], replicated, may hold values from -2 to 2
- self_out: bfloat16 [512, 512], replicated, may hold values from -0.75 to 0.75
- self_out_bias: bfloat16 [512], replicated, may hold values from -2 to 2
- norm_one_gain: bfloat16 [512], replicated, may hold values from 0.5 to 1.5
- norm_one_bias: bfloat16 [512], replicated, may hold values from -2 to 2
- cross_query: bfloat16 [512, 512], replicated, may hold values from -0.25 to 0.25
- cross_query_bias: bfloat16 [512], replicated, may hold values from -2 to 2
- cross_key: bfloat16 [512, 512], replicated, may hold values from -0.25 to 0.25
- cross_value: bfloat16 [512, 512], replicated, may hold values from -0.25 to 0.25
- cross_value_bias: bfloat16 [512], replicated, may hold values from -2 to 2
- cross_out: bfloat16 [512, 512], replicated, may hold values from -1 to 1
- cross_out_bias: bfloat16 [512], replicated, may hold values from -2 to 2
- norm_two_gain: bfloat16 [512], replicated, may hold values from 0.5 to 1.5
- norm_two_bias: bfloat16 [512], replicated, may hold values from -2 to 2
- expand_weight: bfloat16 [512, 3200], replicated, may hold values from -0.25 to 0.25
- expand_bias: bfloat16 [3200], replicated, may hold values from -3 to 3
- project_weight: bfloat16 [3200, 512], replicated, may hold values from -0.109375 to 0.109375
- project_bias: bfloat16 [512], replicated, may hold values from -2 to 2
- norm_three_gain: bfloat16 [512], replicated, may hold values from 0.5 to 1.5
- norm_three_bias: bfloat16 [512], replicated, may hold values from -2 to 2
- out_cotangent: bfloat16 [64, 100, 512], P('ba', 'pb'), may hold values from -6 to 6
Outputs:
- layer_output: bfloat16 [64, 100, 512], P('ba', 'pb')
- input_grad: bfloat16 [64, 100, 512], P('ba', 'pb')
- memory_grad: bfloat16 [64, 1208, 512], P('ba', 'pb')
- embed_grad: float32 [100, 512], P('pb', 'ba')
- self_query_grad: float32 [512, 512], P('ba', 'pb')
- self_query_bias_grad: float32 [512], replicated
- self_key_grad: float32 [512, 512], P('ba', 'pb')
- self_value_grad: float32 [512, 512], P('ba', 'pb')
- self_value_bias_grad: float32 [512], replicated
- self_out_grad: float32 [512, 512], P('ba', 'pb')
- self_out_bias_grad: float32 [512], replicated
- norm_one_gain_grad: float32 [512], replicated
- norm_one_bias_grad: float32 [512], replicated
- cross_query_grad: float32 [512, 512], P('ba', 'pb')
- cross_query_bias_grad: float32 [512], replicated
- cross_key_grad: float32 [512, 512], P('ba', 'pb')
- cross_value_grad: float32 [512, 512], P('ba', 'pb')
- cross_value_bias_grad: float32 [512], replicated
- cross_out_grad: float32 [512, 512], P('ba', 'pb')
- cross_out_bias_grad: float32 [512], replicated
- norm_two_gain_grad: float32 [512], replicated
- norm_two_bias_grad: float32 [512], replicated
- expand_weight_grad: float32 [512, 3200], P('ba', 'pb')
- expand_bias_grad: float32 [3200], replicated
- project_weight_grad: float32 [3200, 512], P('pb', 'ba')
- project_bias_grad: float32 [512], replicated
- norm_three_gain_grad: float32 [512], replicated
- norm_three_bias_grad: float32 [512], replicated
Inputs may be any that keep to these rules, and one draw needn't show every extreme that they name: `lengths`: every length is 302 or 1208; among the 8 items of each index of ba at least one has 1208.
All inputs are finite; a program needn't handle non-finite values.
Results may differ from a plain program's by a relative error of at most 0.025.
The roundings to bfloat16 on the way count: a program that leaves them out, or rounds other values in their place, can miss the bound.
Values may be sent and summed in bfloat16 or wider, within the bound.
No kernel may reach another device: no remote copies, remote signals or barrier semaphores. Data moves between devices by JAX's collectives and lax.ppermute only.
A program may use at most 192 MiB of HBM per device.

v0:
```python
import math

import jax
import jax.numpy as jnp
from jax import lax
from jax.sharding import PartitionSpec as P

HEADS = 8


def sinusoid(first, count, model_width):
    position = (first + jnp.arange(count, dtype=jnp.int32)).astype(jnp.float32)
    column = jnp.arange(model_width // 2, dtype=jnp.int32).astype(jnp.float32)
    frequency = jnp.exp(column * (-2.0 * math.log(10000.0) / model_width))
    angles = position[:, None] * frequency[None, :]
    return jnp.stack([jnp.sin(angles), jnp.cos(angles)], axis=-1).reshape(count, model_width)


def layer_norm(values, norm_gain, norm_shift):
    average = jnp.mean(values, axis=-1, keepdims=True)
    centred = values - average
    spread = jnp.mean(centred * centred, axis=-1, keepdims=True)
    return centred * lax.rsqrt(spread + 1e-05) * norm_gain + norm_shift


def gelu_exact(values):
    return jax.nn.gelu(values, approximate=False)


def linear(left, right):
    return jnp.dot(left, right, preferred_element_type=jnp.float32)


def back_linear(grad_rows, weight):
    return jnp.einsum("bne,de->bnd", grad_rows, weight, preferred_element_type=jnp.float32)


def outer_sum(left, grad_rows):
    return jnp.einsum("bnd,bne->de", left, grad_rows, preferred_element_type=jnp.float32)


def column_sum(grad_rows):
    return jnp.sum(grad_rows.astype(jnp.float32), axis=(0, 1))


def split_heads(values):
    return values.reshape(values.shape[0], values.shape[1], HEADS, values.shape[2] // HEADS)


def join_heads(values):
    return values.reshape(values.shape[0], values.shape[1], values.shape[2] * values.shape[3])


def scores_of(queries, key_rows, score_scale, visible):
    logits = (
        jnp.einsum("bqhd,bkhd->bhqk", queries, key_rows, preferred_element_type=jnp.float32)
        * score_scale
    )
    if visible is not None:
        logits = jnp.where(visible[:, None, None, :], logits, -1e30)
    return logits


def attend(queries, key_rows, value_rows, score_scale):
    logits = scores_of(queries, key_rows, score_scale, None)
    highest = jnp.max(logits, axis=-1, keepdims=True)
    log_total = jnp.log(jnp.sum(jnp.exp(logits - highest), axis=-1, keepdims=True)) + highest
    weights = jnp.exp(logits - log_total).astype(jnp.bfloat16)
    result = jnp.einsum("bhqk,bkhd->bqhd", weights, value_rows, preferred_element_type=jnp.float32)
    return (join_heads(result).astype(jnp.bfloat16), log_total)


def attend_back(queries, key_rows, value_rows, score_scale, log_total, grad_out):
    logits = scores_of(queries, key_rows, score_scale, None)
    weights = jnp.exp(logits - log_total)
    grad_weights = jnp.einsum(
        "bqhd,bkhd->bhqk", grad_out, value_rows, preferred_element_type=jnp.float32
    )
    inner = jnp.sum(weights * grad_weights, axis=-1, keepdims=True)
    grad_logits = (weights * (grad_weights - inner)).astype(jnp.bfloat16)
    grad_queries = (
        jnp.einsum("bhqk,bkhd->bqhd", grad_logits, key_rows, preferred_element_type=jnp.float32)
        * score_scale
    )
    grad_keys = (
        jnp.einsum("bhqk,bqhd->bkhd", grad_logits, queries, preferred_element_type=jnp.float32)
        * score_scale
    )
    grad_values = jnp.einsum(
        "bhqk,bqhd->bkhd",
        weights.astype(jnp.bfloat16),
        grad_out,
        preferred_element_type=jnp.float32,
    )
    return (join_heads(grad_queries), join_heads(grad_keys), join_heads(grad_values))


def local(
    decoder_input,
    memory,
    lengths,
    query_embed,
    self_query,
    self_query_bias,
    self_key,
    self_value,
    self_value_bias,
    self_out,
    self_out_bias,
    norm_one_gain,
    norm_one_bias,
    cross_query,
    cross_query_bias,
    cross_key,
    cross_value,
    cross_value_bias,
    cross_out,
    cross_out_bias,
    norm_two_gain,
    norm_two_bias,
    expand_weight,
    expand_bias,
    project_weight,
    project_bias,
    norm_three_gain,
    norm_three_bias,
    out_cotangent,
):
    model_width = decoder_input.shape[2]
    local_queries = decoder_input.shape[1]
    memory_length = memory.shape[1]
    group_size = lax.axis_size("pb")
    quarter = memory_length // group_size
    offset = lax.axis_index("pb") * quarter
    score_scale = (model_width // HEADS) ** (-0.5)
    embed = query_embed.astype(jnp.float32)
    inputs = decoder_input.astype(jnp.float32)
    attn_input = (inputs + embed[None]).astype(jnp.bfloat16)
    self_queries = (linear(attn_input, self_query) + self_query_bias.astype(jnp.float32)).astype(
        jnp.bfloat16
    )
    self_keys = linear(attn_input, self_key).astype(jnp.bfloat16)
    self_values = (linear(decoder_input, self_value) + self_value_bias.astype(jnp.float32)).astype(
        jnp.bfloat16
    )
    all_keys, all_values = (
        lax.all_gather(self_keys, "pb", axis=1, tiled=True),
        lax.all_gather(self_values, "pb", axis=1, tiled=True),
    )
    self_result, self_log_total = attend(
        split_heads(self_queries), split_heads(all_keys), split_heads(all_values), score_scale
    )
    first_sum = inputs + linear(self_result, self_out) + self_out_bias.astype(jnp.float32)
    first_normed, norm_one_back = jax.vjp(
        layer_norm, first_sum, norm_one_gain.astype(jnp.float32), norm_one_bias.astype(jnp.float32)
    )
    cross_input = (first_normed + embed[None]).astype(jnp.bfloat16)
    cross_queries = (
        linear(cross_input, cross_query) + cross_query_bias.astype(jnp.float32)
    ).astype(jnp.bfloat16)
    memory_part = lax.dynamic_slice_in_dim(memory, offset, quarter, 1)
    keyed_part = (
        memory_part.astype(jnp.float32) + sinusoid(offset, quarter, model_width)[None]
    ).astype(jnp.bfloat16)
    memory_keys = linear(keyed_part, cross_key).astype(jnp.bfloat16)
    memory_values = (
        linear(memory_part, cross_value) + cross_value_bias.astype(jnp.float32)
    ).astype(jnp.bfloat16)
    visible = (offset + jnp.arange(quarter, dtype=jnp.int32))[None, :] < lengths[:, None]
    every_query = lax.all_gather(cross_queries, "pb", axis=1, tiled=True)
    logits = scores_of(split_heads(every_query), split_heads(memory_keys), score_scale, visible)
    highest = jnp.max(logits, axis=-1, keepdims=True)
    part_total = jnp.log(jnp.sum(jnp.exp(logits - highest), axis=-1, keepdims=True)) + highest
    every_total = lax.all_gather(part_total[None], "pb", axis=0, tiled=True)
    top_total = jnp.max(every_total, axis=0)
    cross_log_total = jnp.log(jnp.sum(jnp.exp(every_total - top_total[None]), axis=0)) + top_total
    weights = jnp.exp(logits - cross_log_total).astype(jnp.bfloat16)
    partial_value = join_heads(
        jnp.einsum(
            "bhqk,bkhd->bqhd",
            weights,
            split_heads(memory_values),
            preferred_element_type=jnp.float32,
        )
    )
    cross_result = lax.psum_scatter(
        partial_value.astype(jnp.bfloat16), "pb", scatter_dimension=1, tiled=True
    )
    second_sum = first_normed + linear(cross_result, cross_out) + cross_out_bias.astype(jnp.float32)
    second_normed, norm_two_back = jax.vjp(
        layer_norm, second_sum, norm_two_gain.astype(jnp.float32), norm_two_bias.astype(jnp.float32)
    )
    second_low = second_normed.astype(jnp.bfloat16)
    hidden_pre = linear(second_low, expand_weight) + expand_bias.astype(jnp.float32)
    hidden_act, gelu_back = jax.vjp(gelu_exact, hidden_pre)
    hidden_low = hidden_act.astype(jnp.bfloat16)
    third_sum = (
        second_normed + linear(hidden_low, project_weight) + project_bias.astype(jnp.float32)
    )
    final_normed, norm_three_back = jax.vjp(
        layer_norm,
        third_sum,
        norm_three_gain.astype(jnp.float32),
        norm_three_bias.astype(jnp.float32),
    )
    layer_output = final_normed.astype(jnp.bfloat16)
    third_grad, grad_gain_three, grad_bias_three = norm_three_back(
        out_cotangent.astype(jnp.float32)
    )
    branch_grad = third_grad.astype(jnp.bfloat16)
    grad_project_bias = column_sum(branch_grad)
    grad_project = outer_sum(hidden_low, branch_grad)
    (hidden_grad,) = gelu_back(back_linear(branch_grad, project_weight))
    hidden_grad = hidden_grad.astype(jnp.bfloat16)
    grad_expand_bias = column_sum(hidden_grad)
    grad_expand = outer_sum(second_low, hidden_grad)
    second_grad = third_grad + back_linear(hidden_grad, expand_weight)
    cross_sum_grad, grad_gain_two, grad_bias_two = norm_two_back(second_grad)
    cross_branch = cross_sum_grad.astype(jnp.bfloat16)
    grad_cross_out_bias = column_sum(cross_branch)
    grad_cross_out = outer_sum(cross_result, cross_branch)
    cross_result_grad = back_linear(cross_branch, cross_out).astype(jnp.bfloat16)
    every_result_grad = split_heads(lax.all_gather(cross_result_grad, "pb", axis=1, tiled=True))
    query_heads = split_heads(every_query)
    key_heads = split_heads(memory_keys)
    logits = scores_of(query_heads, key_heads, score_scale, visible)
    weights = jnp.exp(logits - cross_log_total)
    grad_weights = jnp.einsum(
        "bqhd,bkhd->bhqk",
        every_result_grad,
        split_heads(memory_values),
        preferred_element_type=jnp.float32,
    )
    part_inner = jnp.sum(weights * grad_weights, axis=-1, keepdims=True)
    inner = lax.psum(part_inner, "pb")
    grad_logits = (weights * (grad_weights - inner)).astype(jnp.bfloat16)
    query_part = join_heads(
        jnp.einsum("bhqk,bkhd->bqhd", grad_logits, key_heads, preferred_element_type=jnp.float32)
        * score_scale
    )
    cross_query_grad = lax.psum_scatter(
        query_part.astype(jnp.bfloat16), "pb", scatter_dimension=1, tiled=True
    ).astype(jnp.float32)
    memory_key_grad = join_heads(
        jnp.einsum("bhqk,bqhd->bkhd", grad_logits, query_heads, preferred_element_type=jnp.float32)
        * score_scale
    ).astype(jnp.bfloat16)
    memory_value_grad = join_heads(
        jnp.einsum(
            "bhqk,bqhd->bkhd",
            weights.astype(jnp.bfloat16),
            every_result_grad,
            preferred_element_type=jnp.float32,
        )
    ).astype(jnp.bfloat16)
    grad_cross_key = outer_sum(keyed_part, memory_key_grad)
    grad_cross_value = outer_sum(memory_part, memory_value_grad)
    grad_cross_value_bias = column_sum(memory_value_grad)
    memory_grad = (
        back_linear(memory_key_grad, cross_key) + back_linear(memory_value_grad, cross_value)
    ).astype(jnp.bfloat16)
    cross_query_grad = cross_query_grad.astype(jnp.bfloat16)
    grad_cross_query_bias = column_sum(cross_query_grad)
    grad_cross_query = outer_sum(cross_input, cross_query_grad)
    cross_input_grad = back_linear(cross_query_grad, cross_query)
    first_grad = cross_sum_grad + cross_input_grad
    self_sum_grad, grad_gain_one, grad_bias_one = norm_one_back(first_grad)
    self_branch = self_sum_grad.astype(jnp.bfloat16)
    grad_self_out_bias = column_sum(self_branch)
    grad_self_out = outer_sum(self_result, self_branch)
    self_result_grad = back_linear(self_branch, self_out).astype(jnp.bfloat16)
    self_query_grad, self_key_part, self_value_part = attend_back(
        split_heads(self_queries),
        split_heads(all_keys),
        split_heads(all_values),
        score_scale,
        self_log_total,
        split_heads(self_result_grad),
    )
    self_key_grad, self_value_grad = (
        lax.psum_scatter(
            self_key_part.astype(jnp.bfloat16), "pb", scatter_dimension=1, tiled=True
        ).astype(jnp.float32),
        lax.psum_scatter(
            self_value_part.astype(jnp.bfloat16), "pb", scatter_dimension=1, tiled=True
        ).astype(jnp.float32),
    )
    self_key_grad = self_key_grad.astype(jnp.bfloat16)
    self_value_grad = self_value_grad.astype(jnp.bfloat16)
    self_query_grad = self_query_grad.astype(jnp.bfloat16)
    grad_self_query = outer_sum(attn_input, self_query_grad)
    grad_self_query_bias = column_sum(self_query_grad)
    grad_self_key = outer_sum(attn_input, self_key_grad)
    grad_self_value = outer_sum(decoder_input, self_value_grad)
    grad_self_value_bias = column_sum(self_value_grad)
    attn_input_grad = back_linear(self_query_grad, self_query) + back_linear(
        self_key_grad, self_key
    )
    input_grad = (
        self_sum_grad + attn_input_grad + back_linear(self_value_grad, self_value)
    ).astype(jnp.bfloat16)
    embed_local = jnp.sum(attn_input_grad + cross_input_grad, axis=0)
    embed_whole = lax.dynamic_update_slice_in_dim(
        jnp.zeros((local_queries * group_size, model_width), jnp.float32),
        embed_local,
        lax.axis_index("pb") * local_queries,
        0,
    )
    item_summed = (
        lax.psum_scatter(embed_whole, "ba", scatter_dimension=1, tiled=True),
        lax.psum_scatter(grad_self_query, "ba", scatter_dimension=0, tiled=True),
        lax.psum_scatter(grad_self_key, "ba", scatter_dimension=0, tiled=True),
        lax.psum_scatter(grad_self_value, "ba", scatter_dimension=0, tiled=True),
        lax.psum_scatter(grad_self_out, "ba", scatter_dimension=0, tiled=True),
        lax.psum_scatter(grad_cross_query, "ba", scatter_dimension=0, tiled=True),
        lax.psum_scatter(grad_cross_key, "ba", scatter_dimension=0, tiled=True),
        lax.psum_scatter(grad_cross_value, "ba", scatter_dimension=0, tiled=True),
        lax.psum_scatter(grad_cross_out, "ba", scatter_dimension=0, tiled=True),
        lax.psum_scatter(grad_expand, "ba", scatter_dimension=0, tiled=True),
        lax.psum_scatter(grad_project, "ba", scatter_dimension=1, tiled=True),
    )
    (
        embed_grad,
        self_query_out,
        self_key_out,
        self_value_out,
        self_out_out,
        cross_query_out,
        cross_key_out,
        cross_value_out,
        cross_out_out,
        expand_out,
        project_out,
    ) = (
        lax.psum_scatter(
            item_summed[0].astype(jnp.bfloat16), "pb", scatter_dimension=0, tiled=True
        ).astype(jnp.float32),
        lax.psum_scatter(
            item_summed[1].astype(jnp.bfloat16), "pb", scatter_dimension=1, tiled=True
        ).astype(jnp.float32),
        lax.psum_scatter(
            item_summed[2].astype(jnp.bfloat16), "pb", scatter_dimension=1, tiled=True
        ).astype(jnp.float32),
        lax.psum_scatter(
            item_summed[3].astype(jnp.bfloat16), "pb", scatter_dimension=1, tiled=True
        ).astype(jnp.float32),
        lax.psum_scatter(
            item_summed[4].astype(jnp.bfloat16), "pb", scatter_dimension=1, tiled=True
        ).astype(jnp.float32),
        lax.psum_scatter(
            item_summed[5].astype(jnp.bfloat16), "pb", scatter_dimension=1, tiled=True
        ).astype(jnp.float32),
        lax.psum_scatter(
            item_summed[6].astype(jnp.bfloat16), "pb", scatter_dimension=1, tiled=True
        ).astype(jnp.float32),
        lax.psum_scatter(
            item_summed[7].astype(jnp.bfloat16), "pb", scatter_dimension=1, tiled=True
        ).astype(jnp.float32),
        lax.psum_scatter(
            item_summed[8].astype(jnp.bfloat16), "pb", scatter_dimension=1, tiled=True
        ).astype(jnp.float32),
        lax.psum_scatter(
            item_summed[9].astype(jnp.bfloat16), "pb", scatter_dimension=1, tiled=True
        ).astype(jnp.float32),
        lax.psum_scatter(
            item_summed[10].astype(jnp.bfloat16), "pb", scatter_dimension=0, tiled=True
        ).astype(jnp.float32),
    )
    (
        query_bias_out,
        value_bias_out,
        out_bias_out,
        gain_one_out,
        bias_one_out,
        cross_query_bias_out,
        cross_value_bias_out,
        cross_out_bias_out,
        gain_two_out,
        bias_two_out,
        expand_bias_out,
        project_bias_out,
        gain_three_out,
        bias_three_out,
    ) = lax.psum(
        (
            grad_self_query_bias,
            grad_self_value_bias,
            grad_self_out_bias,
            grad_gain_one,
            grad_bias_one,
            grad_cross_query_bias,
            grad_cross_value_bias,
            grad_cross_out_bias,
            grad_gain_two,
            grad_bias_two,
            grad_expand_bias,
            grad_project_bias,
            grad_gain_three,
            grad_bias_three,
        ),
        ("ba", "pb"),
    )
    return (
        layer_output,
        input_grad,
        memory_grad,
        embed_grad,
        self_query_out,
        query_bias_out,
        self_key_out,
        self_value_out,
        value_bias_out,
        self_out_out,
        out_bias_out,
        gain_one_out,
        bias_one_out,
        cross_query_out,
        cross_query_bias_out,
        cross_key_out,
        cross_value_out,
        cross_value_bias_out,
        cross_out_out,
        cross_out_bias_out,
        gain_two_out,
        bias_two_out,
        expand_out,
        expand_bias_out,
        project_out,
        project_bias_out,
        gain_three_out,
        bias_three_out,
    )


def solution(mesh):
    placed = (
        P("ba", "pb", None),
        P("ba", None, None),
        P("ba"),
        P("pb", None),
        P(),
        P(),
        P(),
        P(),
        P(),
        P(),
        P(),
        P(),
        P(),
        P(),
        P(),
        P(),
        P(),
        P(),
        P(),
        P(),
        P(),
        P(),
        P(),
        P(),
        P(),
        P(),
        P(),
        P(),
        P("ba", "pb", None),
    )
    return jax.shard_map(
        local,
        mesh=mesh,
        in_specs=placed,
        out_specs=(
            P("ba", "pb", None),
            P("ba", "pb", None),
            P("ba", "pb", None),
            P("pb", "ba"),
            P("ba", "pb"),
            P(),
            P("ba", "pb"),
            P("ba", "pb"),
            P(),
            P("ba", "pb"),
            P(),
            P(),
            P(),
            P("ba", "pb"),
            P(),
            P("ba", "pb"),
            P("ba", "pb"),
            P(),
            P("ba", "pb"),
            P(),
            P(),
            P(),
            P("ba", "pb"),
            P(),
            P("pb", "ba"),
            P(),
            P(),
            P(),
        ),
        check_vma=False,
    )
```

profile of v0, /device:TPU:0, one launch (start us, length us, event | category | flops | bytes accessed | tf_op | source)
XLA Modules:
  0.0 1386.5 jit_solution(8588494072073840068)
XLA Ops:
  9.9 10.7 all_gather.16
  20.6 2.6 copy.130
  31.4 9.3 all_gather.15
  40.8 2.6 copy.127
  43.4 2.3 fusion.27
  51.8 9.6 all_gather.17
  61.4 2.6 copy.136
  64.0 11.6 multiply_sine_fusion
  77.3 2.5 add.328
  82.1 4.9 convolution_convert_fusion.1
  87.0 4.6 copy.138
  91.7 5.0 fusion.1
  96.7 3.4 exponential_reduce_fusion
  100.5 5.8 all-gather
  106.4 4.7 add_convert_fusion.2
  111.1 4.5 copy.134
  115.7 8.6 convolution_convert_fusion.3
  124.3 2.6 copy.139
  127.1 24.3 %reduce-scatter.50.cloned.1.call-done = bf16[8,25,512]{2,0,1:T(8,128)(2,1)} async-done(((bf16[8,100,512]{2,0,1:T(8,128)(2,1)}), bf16[8,25,512]{2,0,1:T(8,128)(2,1)}) %reduce-scatter.50.cloned.1.call-update) | async-done | bytes 204816 | tf_op jit(solution)/shard_map/reduce_scatter | solution.py:186
  155.1 7.3 multiply_convert_fusion.2
  166.5 2.6 convert_reduce_fusion.1
  173.2 8.8 all_gather.19
  182.0 2.6 copy.143
  184.6 8.9 multiply_reduce_fusion
  193.5 11.3 psum.105
  204.8 8.4 multiply_convert_fusion
  213.2 2.6 multiply_convert_fusion.4
  215.8 2.6 copy.144
  218.5 24.1 %reduce-scatter.52.cloned.1.call-done = bf16[8,25,512]{2,0,1:T(8,128)(2,1)} async-done(((bf16[8,100,512]{2,0,1:T(8,128)(2,1)}), bf16[8,25,512]{2,0,1:T(8,128)(2,1)}) %reduce-scatter.52.cloned.1.call-update) | async-done | bytes 204816 | tf_op jit(solution)/shard_map/reduce_scatter | solution.py:241
  242.6 3.2 multiply_reduce_fusion.3
  253.8 2.6 copy.151
  258.2 2.6 copy.154
  261.1 7.8 convert_reduce_fusion
  270.5 4.7 fusion.23
  276.8 4.4 multiply_convert_fusion.1
  282.8 4.7 fusion.22
  293.3 2.3 convolution_bitcast_fusion.3
  295.9 10.1 reduce-scatter.56.cloned.1.call-done
  308.9 5.3 convolution_bitcast_fusion.1
  315.7 3.8 convolution_bitcast_fusion
  319.6 53.2 %reduce-scatter.70.cloned.1.call-done = f32[64,512]{1,0:T(8,128)} async-done(((f32[512,512]{1,0:T(8,128)}), f32[64,512]{1,0:T(8,128)}) %reduce-scatter.70.cloned.1.call-update) | async-done | bytes 131088 | tf_op jit(solution)/shard_map/reduce_scatter | solution.py:317
  374.6 64.3 %reduce-scatter.72.cloned.1.call-done = f32[64,512]{1,0:T(8,128)} async-done(((f32[512,512]{1,0:T(8,128)}), f32[64,512]{1,0:T(8,128)}) %reduce-scatter.72.cloned.1.call-update) | async-done | bytes 131088 | tf_op jit(solution)/shard_map/reduce_scatter | solution.py:318
  441.0 63.8 %reduce-scatter.68.cloned.1.call-done = f32[64,512]{1,0:T(8,128)} async-done(((f32[512,512]{1,0:T(8,128)}), f32[64,512]{1,0:T(8,128)}) %reduce-scatter.68.cloned.1.call-update) | async-done | bytes 131088 | tf_op jit(solution)/shard_map/reduce_scatter | solution.py:316
  511.9 59.1 %reduce-scatter.66.cloned.1.call-done = f32[64,512]{1,0:T(8,128)} async-done(((f32[512,512]{1,0:T(8,128)}), f32[64,512]{1,0:T(8,128)}) %reduce-scatter.66.cloned.1.call-update) | async-done | bytes 131088 | tf_op jit(solution)/shard_map/reduce_scatter | solution.py:315
  572.8 64.3 %reduce-scatter.64.cloned.1.call-done = f32[64,512]{1,0:T(8,128)} async-done(((f32[512,512]{1,0:T(8,128)}), f32[64,512]{1,0:T(8,128)}) %reduce-scatter.64.cloned.1.call-update) | async-done | bytes 131088 | tf_op jit(solution)/shard_map/reduce_scatter | solution.py:314
  638.8 64.4 %reduce-scatter.58.cloned.1.call-done = f32[64,512]{1,0:T(8,128)} async-done(((f32[512,512]{1,0:T(8,128)}), f32[64,512]{1,0:T(8,128)}) %reduce-scatter.58.cloned.1.call-update) | async-done | bytes 131088 | tf_op jit(solution)/shard_map/reduce_scatter | solution.py:311
  705.0 64.2 %reduce-scatter.60.cloned.1.call-done = f32[64,512]{1,0:T(8,128)} async-done(((f32[512,512]{1,0:T(8,128)}), f32[64,512]{1,0:T(8,128)}) %reduce-scatter.60.cloned.1.call-update) | async-done | bytes 131088 | tf_op jit(solution)/shard_map/reduce_scatter | solution.py:312
  770.9 64.4 %reduce-scatter.84.cloned.1.call-done = f32[64,512]{1,0:T(8,128)} async-done(((f32[512,512]{1,0:T(8,128)}), f32[64,512]{1,0:T(8,128)}) %reduce-scatter.84.cloned.1.call-update) | async-done | bytes 131088
  837.1 122.6 %reduce-scatter.74.cloned.1.call-done = f32[64,3200]{1,0:T(8,128)} async-done(((f32[512,3200]{1,0:T(8,128)}), f32[64,3200]{1,0:T(8,128)}) %reduce-scatter.74.cloned.1.call-update) | async-done | bytes 819216 | tf_op jit(solution)/shard_map/reduce_scatter | solution.py:319
  965.1 5.3 fusion.53
  970.4 114.3 %reduce-scatter.76.cloned.1.call-done = f32[3200,64]{0,1:T(8,128)} async-done(((f32[3200,512]{0,1:T(8,128)}), f32[3200,64]{0,1:T(8,128)}) %reduce-scatter.76.cloned.1.call-update) | async-done | bytes 819216 | tf_op jit(solution)/shard_map/reduce_scatter | solution.py:320
  1089.0 6.0 add_convert_fusion
  1095.6 4.7 copy.169
  1103.3 2.4 reduce-scatter.92.cloned.1.call-done
  1107.2 20.5 %reduce-scatter.94.cloned.1.call-done = bf16[128,64]{1,0:T(8,128)(2,1)} async-done(((bf16[512,64]{1,0:T(8,128)(2,1)}), bf16[128,64]{1,0:T(8,128)(2,1)}) %reduce-scatter.94.cloned.1.call-update) | async-done | bytes 16400
  1129.2 21.0 %reduce-scatter.90.cloned.1.call-done = bf16[128,64]{1,0:T(8,128)(2,1)} async-done(((bf16[512,64]{1,0:T(8,128)(2,1)}), bf16[128,64]{1,0:T(8,128)(2,1)}) %reduce-scatter.90.cloned.1.call-update) | async-done | bytes 16400
  1153.5 61.6 %reduce-scatter.78.cloned.1.call-done = f32[64,100]{1,0:T(8,128)} async-done(((f32[512,100]{1,0:T(8,128)}), f32[64,100]{1,0:T(8,128)}) %reduce-scatter.78.cloned.1.call-update) | async-done | bytes 25616
  1216.5 8.0 fusion
  1228.7 40.9 %all-reduce.2 = (f32[512]{0:T(512)}, f32[512]{0:T(512)}, f32[512]{0:T(512)}, f32[512]{0:T(512)}, f32[512]{0:T(512)}, /*index=5*/f32[512]{0:T(512)}, f32[512]{0:T...) all-reduce(f32[512]{0:T(512)} %reduce_sum.359, ...), channel_id=1, replica_groups=mesh['ba'=8,'pb'=4] {'ba','pb'}, use_global_device_ids=true, to_apply=%region_31.32 | all-reduce | flops 9856 | bytes 78848 | tf_op jit(solution)/shard_map/psum | solution.py:384
  1274.1 6.8 reduce-scatter.80.cloned.1.call-done
  1282.3 21.1 %reduce-scatter.82.cloned.1.call-done = bf16[128,64]{1,0:T(8,128)(2,1)} async-done(((bf16[512,64]{1,0:T(8,128)(2,1)}), bf16[128,64]{1,0:T(8,128)(2,1)}) %reduce-scatter.82.cloned.1.call-update) | async-done | bytes 16400
  1305.0 20.7 %reduce-scatter.62.cloned.1.call-done = bf16[64,128]{0,1:T(8,128)(2,1)} async-done(((bf16[64,512]{0,1:T(8,128)(2,1)}), bf16[64,128]{0,1:T(8,128)(2,1)}) %reduce-scatter.62.cloned.1.call-update) | async-done | bytes 16400 | tf_op jit(solution)/shard_map/reduce_scatter | solution.py:344
  1327.1 24.5 %reduce-scatter.96.cloned.1.call-done = bf16[800,64]{1,0:T(8,128)(2,1)} async-done(((bf16[3200,64]{1,0:T(8,128)(2,1)}), bf16[800,64]{1,0:T(8,128)(2,1)}) %reduce-scatter.96.cloned.1.call-update) | async-done | bytes 102416
  1353.3 24.4 %reduce-scatter.98.cloned.1.call-done = bf16[800,64]{1,0:T(8,128)(2,1)} async-done(((bf16[3200,64]{1,0:T(8,128)(2,1)}), bf16[800,64]{1,0:T(8,128)(2,1)}) %reduce-scatter.98.cloned.1.call-update) | async-done | bytes 102416
  (348 shorter events, 114.6 us)
Async XLA Ops:
  7.2 146.1 %copy-start = (bf16[512,3200]{1,0:T(8,128)(2,1)S(1)}, bf16[512,3200]{1,0:T(8,128)(2,1)}, u32[]{:S(2)}) copy-start(bf16[512,3200]{1,0:T(8,128)(2,1)} %param.51) | copy-start | bytes 9830404
  7.2 16.0 %copy-start.41 = (bf16[8,25,512]{2,0,1:T(8,128)(2,1)S(1)}, bf16[8,25,512]{2,0,1:T(8,128)(2,1)}, u32[]{:S(2)}) copy-start(bf16[8,25,512]{2,0,1:T(8,128)(2,1)} %param.29) | copy-start | bytes 614404
  7.2 16.0 %copy-start.62 = (bf16[512]{0:T(512)(128)(2,1)S(1)}, bf16[512]{0:T(512)(128)(2,1)}, u32[]{:S(2)}) copy-start(bf16[512]{0:T(512)(128)(2,1)} %param.34) | copy-start | bytes 3076
  7.2 144.1 %reduce-scatter.50.cloned.1.call-start = ((), (), s32[]{:S(2)}) async-start(), calls=%async_computation.25 | async-start | bytes 1024000 | tf_op jit(solution)/shard_map/reduce_scatter | solution.py:186
  30.9 14.7 %copy-start.34 = (f32[8,8,25]{2,1,0:T(8,128)}, f32[8,8,25]{2,1,0:T(8,128)S(1)}, u32[]{:S(2)}) copy-start(f32[8,8,25]{2,1,0:T(8,128)S(1)} %log_add_fusion.2) | copy-start | bytes 19204
  47.9 16.1 %copy-start.28 = (bf16[8,25,512]{2,0,1:T(8,128)(2,1)}, bf16[8,25,512]{2,0,1:T(8,128)(2,1)S(1)}, u32[]{:S(2)}) copy-start(bf16[8,25,512]{2,0,1:T(8,128)(2,1)S(1)} %convert_element_type.329) | copy-start | bytes 614404
  49.7 101.6 %copy-start.50 = (f32[512]{0:T(512)}, f32[512]{0:T(512)S(1)}, u32[]{:S(2)}) copy-start(f32[512]{0:T(512)S(1)} %convert_element_type.331) | copy-start | bytes 6148
  49.8 101.6 %copy-start.58 = (f32[512]{0:T(512)}, f32[512]{0:T(512)S(1)}, u32[]{:S(2)}) copy-start(f32[512]{0:T(512)S(1)} %convert_element_type.332) | copy-start | bytes 6148
  115.7 11.3 copy-start.71
  115.7 11.3 copy-start.57
  115.7 11.4 copy-start.72
  115.7 11.4 copy-start.73
  115.7 11.4 copy-start.74
  126.9 115.7 %reduce-scatter.52.cloned.1.call-start = ((), (), s32[]{:S(2)}) async-start(), calls=%async_computation.26 | async-start | bytes 1024000 | tf_op jit(solution)/shard_map/reduce_scatter | solution.py:241
  127.0 43.9 %copy-start.54 = (f32[512]{0:T(512)}, f32[512]{0:T(512)S(1)}, u32[]{:S(2)}) copy-start(f32[512]{0:T(512)S(1)} %convert_element_type.348) | copy-start | bytes 6148
  127.0 35.5 %copy-start.60 = (f32[512]{0:T(512)}, f32[512]{0:T(512)S(1)}, u32[]{:S(2)}) copy-start(f32[512]{0:T(512)S(1)} %convert_element_type.349) | copy-start | bytes 6148
  153.0 17.9 %copy-start.18 = (f32[8,25,512]{2,1,0:T(8,128)}, f32[8,25,512]{2,1,0:T(8,128)S(1)}, u32[]{:S(2)}) copy-start(f32[8,25,512]{2,1,0:T(8,128)S(1)} %get-tuple-element.164) | copy-start | bytes 1228804
  153.1 17.9 %copy-start.48 = (f32[8,25]{1,0:T(8,128)}, f32[8,25]{1,0:T(8,128)S(1)}, u32[]{:S(2)}) copy-start(f32[8,25]{1,0:T(8,128)S(1)} %broadcast_multiply_fusion.1) | copy-start | bytes 2404
  153.3 17.6 %copy-start.52 = (f32[8,25]{1,0:T(8,128)}, f32[8,25]{1,0:T(8,128)S(1)}, u32[]{:S(2)}) copy-start(f32[8,25]{1,0:T(8,128)S(1)} %fusion.95) | copy-start | bytes 2404
  170.9 13.7 copy-start.11
  170.9 13.7 copy-start.45
  213.2 29.4 %copy-start.51 = (f32[512]{0:T(512)S(1)}, f32[512]{0:T(512)}, u32[]{:S(2)}) copy-start(f32[512]{0:T(512)} %copy-done.50) | copy-start | bytes 6148
  215.8 30.0 %copy-start.8 = (f32[8,25,512]{2,1,0:T(8,128)S(1)}, f32[8,25,512]{2,1,0:T(8,128)}, u32[]{:S(2)}) copy-start(f32[8,25,512]{2,1,0:T(8,128)} %copy-done.7) | copy-start | bytes 1228804
  218.4 32.4 %copy-start.6 = (f32[8,8,25,100]{3,2,1,0:T(8,128)S(1)}, f32[8,8,25,100]{3,2,1,0:T(8,128)}, u32[]{:S(2)}) copy-start(f32[8,8,25,100]{3,2,1,0:T(8,128)} %copy-done.5) | copy-start | bytes 1920004
  218.4 32.4 %copy-start.12 = (bf16[8,100,512]{1,2,0:T(8,128)(2,1)S(1)}, bf16[8,100,512]{1,2,0:T(8,128)(2,1)}, u32[]{:S(2)}) copy-start(bf16[8,100,512]{1,2,0:T(8,128)(2,1)} %copy.127) | copy-start | bytes 2457604
  218.5 32.4 %copy-start.35 = (f32[8,8,25]{2,1,0:T(8,128)S(1)}, f32[8,8,25]{2,1,0:T(8,128)}, u32[]{:S(2)}) copy-start(f32[8,8,25]{2,1,0:T(8,128)} %copy-done.34) | copy-start | bytes 19204
  218.5 74.8 %reduce-scatter.54.cloned.1.call-start = ((), (), s32[]{:S(2)}) async-start(), calls=%async_computation.27 | async-start | bytes 1024000 | tf_op jit(solution)/shard_map/reduce_scatter | solution.py:281
  256.4 49.7 %reduce-scatter.56.cloned.1.call-start = ((), (), s32[]{:S(2)}) async-start(), calls=%async_computation.28 | async-start | bytes 1024000 | tf_op jit(solution)/shard_map/reduce_scatter | solution.py:284
  260.8 112.0 %reduce-scatter.70.cloned.1.call-start = ((), (), s32[]{:S(2)}) async-start(), calls=%async_computation.35 | async-start | bytes 1179648 | tf_op jit(solution)/shard_map/reduce_scatter | solution.py:317
  275.2 163.7 %reduce-scatter.72.cloned.1.call-start = ((), (), s32[]{:S(2)}) async-start(), calls=%async_computation.36 | async-start | bytes 1179648 | tf_op jit(solution)/shard_map/reduce_scatter | solution.py:318
  276.7 228.1 %reduce-scatter.68.cloned.1.call-start = ((), (), s32[]{:S(2)}) async-start(), calls=%async_computation.34 | async-start | bytes 1179648 | tf_op jit(solution)/shard_map/reduce_scatter | solution.py:316
  287.5 283.6 %reduce-scatter.66.cloned.1.call-start = ((), (), s32[]{:S(2)}) async-start(), calls=%async_computation.33 | async-start | bytes 1179648 | tf_op jit(solution)/shard_map/reduce_scatter | solution.py:315
  289.1 348.0 %reduce-scatter.64.cloned.1.call-start = ((), (), s32[]{:S(2)}) async-start(), calls=%async_computation.32 | async-start | bytes 1179648 | tf_op jit(solution)/shard_map/reduce_scatter | solution.py:314
  290.6 412.6 %reduce-scatter.58.cloned.1.call-start = ((), (), s32[]{:S(2)}) async-start(), calls=%async_computation.29 | async-start | bytes 1179648 | tf_op jit(solution)/shard_map/reduce_scatter | solution.py:311
  293.2 476.0 %reduce-scatter.60.cloned.1.call-start = ((), (), s32[]{:S(2)}) async-start(), calls=%async_computation.30 | async-start | bytes 1179648 | tf_op jit(solution)/shard_map/reduce_scatter | solution.py:312
  295.6 13.3 copy-start.19
  295.6 13.3 copy-start.49
  295.6 13.3 copy-start.53
  295.6 13.3 copy-start.55
  295.6 13.2 copy-start.61
  295.6 539.7 %reduce-scatter.84.cloned.1.call-start = ((), (), s32[]{:S(2)}) async-start(), calls=%async_computation.42 | async-start | bytes 1179648
  308.8 650.9 %reduce-scatter.74.cloned.1.call-start = ((), (), s32[]{:S(2)}) async-start(), calls=%async_computation.37 | async-start | bytes 7372800 | tf_op jit(solution)/shard_map/reduce_scatter | solution.py:319
  314.2 770.5 %reduce-scatter.76.cloned.1.call-start = ((), (), s32[]{:S(2)}) async-start(), calls=%async_computation.38 | async-start | bytes 7372800 | tf_op jit(solution)/shard_map/reduce_scatter | solution.py:320
  319.5 121.2 %copy-start.38 = (bf16[512,512]{1,0:T(8,128)(2,1)S(1)}, bf16[512,512]{1,0:T(8,128)(2,1)}, u32[]{:S(2)}) copy-start(bf16[512,512]{1,0:T(8,128)(2,1)} %param.33) | copy-start | bytes 1572868
  319.5 187.0 %copy-start.24 = (f32[8,25,512]{2,1,0:T(8,128)S(1)}, f32[8,25,512]{2,1,0:T(8,128)}, u32[]{:S(2)}) copy-start(f32[8,25,512]{2,1,0:T(8,128)} %get-tuple-element.171) | copy-start | bytes 1228804
  319.5 187.1 %copy-start.37 = (bf16[512,512]{1,0:T(8,128)(2,1)S(1)}, bf16[512,512]{1,0:T(8,128)(2,1)}, u32[]{:S(2)}) copy-start(bf16[512,512]{1,0:T(8,128)(2,1)} %param.35) | copy-start | bytes 1572868
  319.5 187.1 %copy-start.40 = (bf16[8,25,512]{2,0,1:T(8,128)(2,1)S(1)}, bf16[8,25,512]{2,0,1:T(8,128)(2,1)}, u32[]{:S(2)}) copy-start(bf16[8,25,512]{2,0,1:T(8,128)(2,1)} %reduce-scatter.54.cloned.1.call-done) | copy-start | bytes 614404
  319.5 786.2 %reduce-scatter.92.cloned.1.call-start = ((), (), s32[]{:S(2)}) async-start(), calls=%async_computation.46 | async-start | bytes 163840
  374.5 753.2 %reduce-scatter.94.cloned.1.call-start = ((), (), s32[]{:S(2)}) async-start(), calls=%async_computation.47 | async-start | bytes 163840
  440.6 709.6 %reduce-scatter.90.cloned.1.call-start = ((), (), s32[]{:S(2)}) async-start(), calls=%async_computation.45 | async-start | bytes 163840
  506.5 708.6 %reduce-scatter.78.cloned.1.call-start = ((), (), s32[]{:S(2)}) async-start(), calls=%async_computation.39 | async-start | bytes 294912
  509.9 454.0 %copy-start.75 = (u32[32]{0:T(128)S(1)}, u32[32]{0:T(128)}, u32[]{:S(2)}) copy-start(u32[32]{0:T(128)} %constant.113) | copy-start | bytes 388
  509.9 455.2 %copy-start.10 = (bf16[8,8,64,302]{3,2,1,0:T(8,128)(2,1)S(1)}, bf16[8,8,64,302]{3,2,1,0:T(8,128)(2,1)}, u32[]{:S(2)}) copy-start(bf16[8,8,64,302]{3,2,1,0:T(8,128)(2,1)} %copy-done.9) | copy-start | bytes 7421956
  511.9 759.2 %reduce-scatter.88.cloned.1.call-start = ((), (), s32[]{:S(2)}) async-start(), calls=%async_computation.44 | async-start | bytes 163840
  572.8 699.8 %reduce-scatter.86.cloned.1.call-start = ((), (), s32[]{:S(2)}) async-start(), calls=%async_computation.43 | async-start | bytes 163840
  638.8 642.1 %reduce-scatter.80.cloned.1.call-start = ((), (), s32[]{:S(2)}) async-start(), calls=%async_computation.40 | async-start | bytes 163840
  704.9 598.6 %reduce-scatter.82.cloned.1.call-start = ((), (), s32[]{:S(2)}) async-start(), calls=%async_computation.41 | async-start | bytes 163840
  770.9 554.8 %reduce-scatter.62.cloned.1.call-start = ((), (), s32[]{:S(2)}) async-start(), calls=%async_computation.31 | async-start | bytes 163840 | tf_op jit(solution)/shard_map/reduce_scatter | solution.py:344
  837.0 514.6 %reduce-scatter.96.cloned.1.call-start = ((), (), s32[]{:S(2)}) async-start(), calls=%async_computation.48 | async-start | bytes 1024000
  963.8 413.9 %reduce-scatter.98.cloned.1.call-start = ((), (), s32[]{:S(2)}) async-start(), calls=%async_computation.49 | async-start | bytes 1024000
  970.4 118.5 %copy-start.23 = (bf16[8,8,64,302]{3,2,1,0:T(8,128)(2,1)S(1)}, bf16[8,8,64,302]{3,2,1,0:T(8,128)(2,1)}, u32[]{:S(2)}) copy-start(bf16[8,8,64,302]{3,2,1,0:T(8,128)(2,1)} %copy-done.22) | copy-start | bytes 7421956
  1095.6 133.1 %copy-start.56 = (f32[512]{0:T(512)S(1)}, f32[512]{0:T(512)}, u32[]{:S(2)}) copy-start(f32[512]{0:T(512)} %get-tuple-element.118) | copy-start | bytes 6148
  1095.6 283.9 %copy-start.1 = (bf16[512,3200]{1,0:T(8,128)(2,1)S(1)}, bf16[512,3200]{1,0:T(8,128)(2,1)}, u32[]{:S(2)}) copy-start(bf16[512,3200]{1,0:T(8,128)(2,1)} %param.51) | copy-start | bytes 9830404
  1225.1 44.6 %collective-permute-start = (bf16[21,64]{1,0:T(8,128)(2,1)}, bf16[21,64]{1,0:T(8,128)(2,1)}, u32[]{:S(2)}, u32[]{:S(2)}) collective-permute-start(bf16[21,64]{1,0:T(8,128)(2,1)} %slice), channel_id=1, source_target_pairs={{0,1},{1,2},{2,3},{4,5},{5,6},{6,7},{8,9},{9,10},{10,11},{12,13},{... | collective-permute-start | bytes 8072
  (41 other events, 162.6 us)
Sparse Core Ops, SparseCore 0:
  127.0 24.3 reduce-scatter.49
  218.6 23.9 reduce-scatter.51
  256.5 23.4 reduce-scatter.53
  282.5 23.4 reduce-scatter.55
  309.3 63.4 reduce-scatter.69
  376.4 62.4 reduce-scatter.71
  442.3 62.4 reduce-scatter.67
  508.6 62.4 reduce-scatter.65
  574.5 62.5 reduce-scatter.63
  640.7 62.4 reduce-scatter.57
  706.6 62.5 reduce-scatter.59
  772.8 62.4 reduce-scatter.83
  838.9 120.6 reduce-scatter.73
  963.6 121.1 reduce-scatter.75
  1087.0 18.6 reduce-scatter.91
  1108.2 19.5 reduce-scatter.93
  1130.6 19.5 reduce-scatter.89
  1153.8 61.2 reduce-scatter.77
  1217.6 18.5 reduce-scatter.87
  1238.5 19.6 reduce-scatter.85
  1261.3 19.5 reduce-scatter.79
  1283.9 19.5 reduce-scatter.81
  1306.0 19.5 reduce-scatter.61
  1328.0 23.4 reduce-scatter.95
  1354.3 23.4 reduce-scatter.97
where the time goes:
time: 1390 us
  waiting for transfers between devices  997 us (72%)
  matrix products  119 us (9%)
  blocking collectives  104 us (7%)
  local copies, waits for them, and re-layouts  87.7 us (6%)
  other arithmetic  58.4 us (4%)
  between operations  16.7 us (1%)
    unnamed x37, waiting for transfers between devices  247 us
    reduce_scatter x1, waiting for transfers between devices, local(): lax.psum_scatter(grad_expand, 'ba', scatter_dimension=0, tiled=True)  123 us
    reduce_scatter x1, waiting for transfers between devices, local(): lax.psum_scatter(grad_project, 'ba', scatter_dimension=1, tiled=True)  114 us
    reduce_scatter x1, waiting for transfers between devices, local(): lax.psum_scatter(grad_self_query, 'ba', scatter_dimension=0, tiled=True)  64.4 us
    reduce_scatter x1, waiting for transfers between devices, local(): lax.psum_scatter(grad_cross_out, 'ba', scatter_dimension=0, tiled=True)  64.3 us
    reduce_scatter x1, waiting for transfers between devices, local(): lax.psum_scatter(grad_self_out, 'ba', scatter_dimension=0, tiled=True)  64.3 us
    reduce_scatter x1, waiting for transfers between devices, local(): lax.psum_scatter(grad_self_key, 'ba', scatter_dimension=0, tiled=True)  64.2 us
    reduce_scatter x1, waiting for transfers between devices, local(): lax.psum_scatter(grad_cross_key, 'ba', scatter_dimension=0, tiled=True)  63.8 us
  transfers between devices with their start and end apart: 26, of which 22 were waited for; matrix products, arithmetic and copies ran while one was open for 9% of the time, Pallas kernels for 0%

commit v1 on v0

v1 whole, which is shorter than its diff:
```python
import math

import jax
import jax.numpy as jnp
import numpy as np
from jax import lax
from jax.sharding import PartitionSpec as P

HEADS = 8


def sinusoid(count, model_width):
    position = np.arange(count, dtype=np.float32)
    column = np.arange(model_width // 2, dtype=np.float32)
    frequency = np.exp(column * np.float32(-2.0 * math.log(10000.0) / model_width)).astype(np.float32)
    angles = (position[:, None] * frequency[None, :]).astype(np.float32)
    table = np.stack([np.sin(angles), np.cos(angles)], axis=-1)
    return table.reshape(count, model_width).astype(np.float32)


def layer_norm(values, norm_gain, norm_shift):
    average = jnp.mean(values, axis=-1, keepdims=True)
    centred = values - average
    spread = jnp.mean(centred * centred, axis=-1, keepdims=True)
    return centred * lax.rsqrt(spread + 1e-05) * norm_gain + norm_shift


def linear(left, right):
    return jnp.dot(left, right, preferred_element_type=jnp.float32)


def back_linear(grad_rows, weight):
    return jnp.einsum("bne,de->bnd", grad_rows, weight, preferred_element_type=jnp.float32)


def outer_sum(left, grad_rows):
    return jnp.einsum("bnd,bne->de", left, grad_rows, preferred_element_type=jnp.float32)


def column_sum(grad_rows):
    return jnp.sum(grad_rows.astype(jnp.float32), axis=(0, 1))


def split_heads(values):
    return values.reshape(values.shape[0], values.shape[1], HEADS, values.shape[2] // HEADS)


def join_heads(values):
    return values.reshape(values.shape[0], values.shape[1], values.shape[2] * values.shape[3])


def attend(queries, key_rows, value_rows, score_scale, visible):
    logits = (
        jnp.einsum("bqhd,bkhd->bhqk", queries, key_rows, preferred_element_type=jnp.float32)
        * score_scale
    )
    if visible is not None:
        logits = jnp.where(visible[:, None, None, :], logits, -1e30)
    highest = jnp.max(logits, axis=-1, keepdims=True)
    raised = jnp.exp(logits - highest)
    weights = raised / jnp.sum(raised, axis=-1, keepdims=True)
    low = weights.astype(jnp.bfloat16)
    result = jnp.einsum("bhqk,bkhd->bqhd", low, value_rows, preferred_element_type=jnp.float32)
    return join_heads(result).astype(jnp.bfloat16), weights


def attend_back(queries, key_rows, value_rows, score_scale, weights, grad_out):
    grad_weights = jnp.einsum(
        "bqhd,bkhd->bhqk", grad_out, value_rows, preferred_element_type=jnp.float32
    )
    inner = jnp.sum(weights * grad_weights, axis=-1, keepdims=True)
    grad_logits = (weights * (grad_weights - inner)).astype(jnp.bfloat16)
    grad_queries = (
        jnp.einsum("bhqk,bkhd->bqhd", grad_logits, key_rows, preferred_element_type=jnp.float32)
        * score_scale
    )
    grad_keys = (
        jnp.einsum("bhqk,bqhd->bkhd", grad_logits, queries, preferred_element_type=jnp.float32)
        * score_scale
    )
    grad_values = jnp.einsum(
        "bhqk,bqhd->bkhd",
        weights.astype(jnp.bfloat16),
        grad_out,
        preferred_element_type=jnp.float32,
    )
    return (
        join_heads(grad_queries).astype(jnp.bfloat16),
        join_heads(grad_keys).astype(jnp.bfloat16),
        join_heads(grad_values).astype(jnp.bfloat16),
    )


def swap(values, axis, bit):
    size = lax.axis_size(axis)
    return lax.ppermute(values, axis, [(i, i ^ bit) for i in range(size)])


def pick(values, index, axis):
    return lax.dynamic_index_in_dim(values, index, axis, keepdims=False)


def halve(values, axis, bit, dim):
    mine = (lax.axis_index(axis) // bit) % 2
    sent = pick(values, 1 - mine, dim)
    kept = pick(values, mine, dim)
    got = swap(sent, axis, bit)
    total = kept.astype(jnp.float32) + got.astype(jnp.float32)
    return total


def reduce_blocks(blocks, order):
    total = blocks.astype(jnp.bfloat16)
    for step, (axis, bit) in enumerate(order):
        total = halve(total, axis, bit, 0)
        if step < len(order) - 1:
            total = total.astype(jnp.bfloat16)
    return total


def bits_of(size):
    return [1 << b for b in range(size.bit_length() - 1)]


def regroup(values, axis_dims, order):
    return values


def to_blocks(grad, row_axis, col_axis, order):
    sizes = {axis: lax.axis_size(axis) for axis in ("ba", "pb")}
    dims = []
    shape = []
    for axis, extent in ((row_axis, grad.shape[0]), (col_axis, grad.shape[1])):
        for bit in reversed(bits_of(sizes[axis])):
            dims.append((axis, bit))
            shape.append(2)
        dims.append((axis, 0))
        shape.append(extent // sizes[axis])
    grad = grad.reshape(shape)
    places = [dims.index(step) for step in order]
    rest = [i for i, d in enumerate(dims) if d[1] == 0]
    return grad.transpose(places + rest)


def exchange(values, axis):
    size = lax.axis_size(axis)
    return [values[0]] + [swap(values[k], axis, k) for k in range(1, size)]


def local(
    decoder_input,
    memory,
    lengths,
    query_embed,
    self_query,
    self_query_bias,
    self_key,
    self_value,
    self_value_bias,
    self_out,
    self_out_bias,
    norm_one_gain,
    norm_one_bias,
    cross_query,
    cross_query_bias,
    cross_key,
    cross_value,
    cross_value_bias,
    cross_out,
    cross_out_bias,
    norm_two_gain,
    norm_two_bias,
    expand_weight,
    expand_bias,
    project_weight,
    project_bias,
    norm_three_gain,
    norm_three_bias,
    out_cotangent,
):
    f32 = jnp.float32
    bf16 = jnp.bfloat16
    items, chunk, model_width = decoder_input.shape
    memory_length = memory.shape[1]
    group = lax.axis_size("pb")
    place = lax.axis_index("pb")
    own = items // group
    quarter = memory_length // group
    score_scale = (model_width // HEADS) ** (-0.5)

    def gather_rows(values):
        parts = [lax.dynamic_slice_in_dim(values, (place ^ k) * own, own, 0) for k in range(group)]
        return jnp.concatenate(exchange(parts, "pb"), axis=1)

    def return_rows(values):
        parts = exchange([values[:, k * chunk : (k + 1) * chunk] for k in range(group)], "pb")
        whole = jnp.zeros((items, chunk, model_width), values.dtype)
        for k in range(group):
            whole = lax.dynamic_update_slice_in_dim(whole, parts[k], (place ^ k) * own, 0)
        return whole

    decoder_rows = gather_rows(decoder_input)
    embed = jnp.concatenate(exchange([query_embed] * group, "pb"), axis=0).astype(f32)
    cotangent_rows = gather_rows(out_cotangent)
    own_memory = lax.dynamic_slice_in_dim(memory, place * own, own, 0)
    own_lengths = lax.dynamic_slice_in_dim(lengths, place * own, own, 0)

    table = jnp.asarray(sinusoid(memory_length, model_width))
    keyed = (own_memory.astype(f32) + table[None]).astype(bf16)
    memory_keys = linear(keyed, cross_key).astype(bf16)
    memory_values = (linear(own_memory, cross_value) + cross_value_bias.astype(f32)).astype(bf16)
    visible = jnp.arange(memory_length, dtype=jnp.int32)[None, :] < own_lengths[:, None]

    inputs = decoder_rows.astype(f32)
    attn_input = (inputs + embed[None]).astype(bf16)
    self_queries = (linear(attn_input, self_query) + self_query_bias.astype(f32)).astype(bf16)
    self_keys = linear(attn_input, self_key).astype(bf16)
    self_values = (linear(decoder_rows, self_value) + self_value_bias.astype(f32)).astype(bf16)
    self_result, self_weights = attend(
        split_heads(self_queries), split_heads(self_keys), split_heads(self_values), score_scale, None
    )
    first_sum = inputs + linear(self_result, self_out) + self_out_bias.astype(f32)
    first_normed, norm_one_back = jax.vjp(
        layer_norm, first_sum, norm_one_gain.astype(f32), norm_one_bias.astype(f32)
    )
    cross_input = (first_normed + embed[None]).astype(bf16)
    cross_queries = (linear(cross_input, cross_query) + cross_query_bias.astype(f32)).astype(bf16)
    cross_result, cross_weights = attend(
        split_heads(cross_queries),
        split_heads(memory_keys),
        split_heads(memory_values),
        score_scale,
        visible,
    )
    second_sum = first_normed + linear(cross_result, cross_out) + cross_out_bias.astype(f32)
    second_normed, norm_two_back = jax.vjp(
        layer_norm, second_sum, norm_two_gain.astype(f32), norm_two_bias.astype(f32)
    )
    second_low = second_normed.astype(bf16)
    hidden_pre = linear(second_low, expand_weight) + expand_bias.astype(f32)
    hidden_act, gelu_back = jax.vjp(lambda v: jax.nn.gelu(v, approximate=False), hidden_pre)
    hidden_low = hidden_act.astype(bf16)
    third_sum = second_normed + linear(hidden_low, project_weight) + project_bias.astype(f32)
    final_normed, norm_three_back = jax.vjp(
        layer_norm, third_sum, norm_three_gain.astype(f32), norm_three_bias.astype(f32)
    )
    layer_output = return_rows(final_normed.astype(bf16))

    third_grad, grad_gain_three, grad_bias_three = norm_three_back(cotangent_rows.astype(f32))
    branch_grad = third_grad.astype(bf16)
    grad_project_bias = column_sum(branch_grad)
    grad_project = outer_sum(hidden_low, branch_grad)
    (hidden_grad,) = gelu_back(back_linear(branch_grad, project_weight))
    hidden_grad = hidden_grad.astype(bf16)
    grad_expand_bias = column_sum(hidden_grad)
    grad_expand = outer_sum(second_low, hidden_grad)

    ba_bits = bits_of(lax.axis_size("ba"))
    pb_bits = bits_of(lax.axis_size("pb"))
    x_first = [("pb", 1), ("ba", 1)] + [("pb", b) for b in pb_bits[1:]] + [("ba", b) for b in ba_bits[1:]]
    y_first = [("pb", b) for b in pb_bits] + [("ba", b) for b in ba_bits]

    project_out = reduce_blocks(to_blocks(grad_project, "pb", "ba", x_first), x_first)
    expand_out = reduce_blocks(to_blocks(grad_expand, "ba", "pb", y_first), y_first)

    second_grad = third_grad + back_linear(hidden_grad, expand_weight)
    cross_sum_grad, grad_gain_two, grad_bias_two = norm_two_back(second_grad)
    cross_branch = cross_sum_grad.astype(bf16)
    grad_cross_out_bias = column_sum(cross_branch)
    grad_cross_out = outer_sum(cross_result, cross_branch)
    cross_result_grad = back_linear(cross_branch, cross_out).astype(bf16)
    cross_query_grad, memory_key_grad, memory_value_grad = attend_back(
        split_heads(cross_queries),
        split_heads(memory_keys),
        split_heads(memory_values),
        score_scale,
        cross_weights,
        split_heads(cross_result_grad),
    )
    grad_cross_key = outer_sum(keyed, memory_key_grad)
    grad_cross_value = outer_sum(own_memory, memory_value_grad)
    grad_cross_value_bias = column_sum(memory_value_grad)
    own_memory_grad = (
        back_linear(memory_key_grad, cross_key) + back_linear(memory_value_grad, cross_value)
    ).astype(bf16)
    parts = exchange(
        [
            lax.dynamic_slice_in_dim(own_memory_grad, (place ^ k) * quarter, quarter, 1)
            for k in range(group)
        ],
        "pb",
    )
    memory_grad = jnp.zeros((items, quarter, model_width), bf16)
    for k in range(group):
        memory_grad = lax.dynamic_update_slice_in_dim(memory_grad, parts[k], (place ^ k) * own, 0)

    grad_cross_query_bias = column_sum(cross_query_grad)
    grad_cross_query = outer_sum(cross_input, cross_query_grad)
    cross_input_grad = back_linear(cross_query_grad, cross_query)
    cross_grads = jnp.stack(
        [
            to_blocks(g, "ba", "pb", x_first)
            for g in (grad_cross_query, grad_cross_key, grad_cross_value, grad_cross_out)
        ],
        axis=len(x_first),
    )
    cross_outs = reduce_blocks(cross_grads, x_first)

    first_grad = cross_sum_grad + cross_input_grad
    self_sum_grad, grad_gain_one, grad_bias_one = norm_one_back(first_grad)
    self_branch = self_sum_grad.astype(bf16)
    grad_self_out_bias = column_sum(self_branch)
    grad_self_out = outer_sum(self_result, self_branch)
    self_result_grad = back_linear(self_branch, self_out).astype(bf16)
    self_query_grad, self_key_grad, self_value_grad = attend_back(
        split_heads(self_queries),
        split_heads(self_keys),
        split_heads(self_values),
        score_scale,
        self_weights,
        split_heads(self_result_grad),
    )
    grad_self_query = outer_sum(attn_input, self_query_grad)
    grad_self_query_bias = column_sum(self_query_grad)
    grad_self_key = outer_sum(attn_input, self_key_grad)
    grad_self_value = outer_sum(decoder_rows, self_value_grad)
    grad_self_value_bias = column_sum(self_value_grad)
    self_grads = jnp.stack(
        [
            to_blocks(g, "ba", "pb", x_first)
            for g in (grad_self_query, grad_self_key, grad_self_value, grad_self_out)
        ],
        axis=len(x_first),
    )
    self_outs = reduce_blocks(self_grads, x_first)

    attn_input_grad = back_linear(self_query_grad, self_query) + back_linear(self_key_grad, self_key)
    input_grad = return_rows(
        (self_sum_grad + attn_input_grad + back_linear(self_value_grad, self_value)).astype(bf16)
    )
    embed_local = jnp.sum(attn_input_grad + cross_input_grad, axis=0)
    embed_local = embed_local.reshape(group, chunk, model_width)
    for bit in pb_bits:
        spread = embed_local.reshape(group // (2 * bit), 2, bit, chunk, model_width)
        embed_local = jnp.where((place // bit) % 2 == 1, spread[:, ::-1], spread).reshape(
            group, chunk, model_width
        )
    embed_local = embed_local.reshape(group * chunk, model_width)
    embed_grad = reduce_blocks(to_blocks(embed_local, "pb", "ba", x_first), x_first)

    vectors = (
        grad_self_query_bias,
        grad_self_value_bias,
        grad_self_out_bias,
        grad_gain_one,
        grad_bias_one,
        grad_cross_query_bias,
        grad_cross_value_bias,
        grad_cross_out_bias,
        grad_gain_two,
        grad_bias_two,
        grad_expand_bias,
        grad_project_bias,
        grad_gain_three,
        grad_bias_three,
    )
    total = jnp.concatenate(vectors).reshape(-1, 128)
    for axis, bit in x_first:
        total = total + swap(total, axis, bit)
    total = total.reshape(-1)
    summed = []
    start = 0
    for v in vectors:
        summed.append(total[start : start + v.shape[0]])
        start += v.shape[0]
    (
        query_bias_out,
        value_bias_out,
        out_bias_out,
        gain_one_out,
        bias_one_out,
        cross_query_bias_out,
        cross_value_bias_out,
        cross_out_bias_out,
        gain_two_out,
        bias_two_out,
        expand_bias_out,
        project_bias_out,
        gain_three_out,
        bias_three_out,
    ) = summed
    return (
        layer_output,
        input_grad,
        memory_grad,
        embed_grad,
        self_outs[0],
        query_bias_out,
        self_outs[1],
        self_outs[2],
        value_bias_out,
        self_outs[3],
        out_bias_out,
        gain_one_out,
        bias_one_out,
        cross_outs[0],
        cross_query_bias_out,
        cross_outs[1],
        cross_outs[2],
        cross_value_bias_out,
        cross_outs[3],
        cross_out_bias_out,
        gain_two_out,
        bias_two_out,
        expand_out,
        expand_bias_out,
        project_out,
        project_bias_out,
        gain_three_out,
        bias_three_out,
    )


def solution(mesh):
    rows = P("ba", "pb", None)
    copied = P()
    placed = (rows, P("ba", None, None), P("ba"), P("pb", None)) + (copied,) * 24 + (rows,)
    square = P("ba", "pb")
    return jax.shard_map(
        local,
        mesh=mesh,
        in_specs=placed,
        out_specs=(
            rows,
            rows,
            rows,
            P("pb", "ba"),
            square,
            copied,
            square,
            square,
            copied,
            square,
            copied,
            copied,
            copied,
            square,
            copied,
            square,
            square,
            copied,
            square,
            copied,
            copied,
            copied,
            square,
            copied,
            P("pb", "ba"),
            copied,
            copied,
            copied,
        ),
        check_vma=False,
    )
```

time: 1390 us -> 448 us (0.32)
  waiting for transfers between devices: 997 us -> 77.9 us
  blocking collectives: 104 us -> 0 us
  local copies, waits for them, and re-layouts: 87.7 us -> 146 us
  starting transfers between devices: 3.37 us -> 45.8 us
  matrix products: 119 us -> 97.3 us
  between operations: 16.7 us -> 2.67 us
    reduce_scatter x14 -> x0, waiting for transfers between devices: 749 us -> none  [the longest x1 123 us: local(): lax.psum_scatter(grad_expand, 'ba', scatter_dimension=0, tiled=True)]
    unnamed x37 -> x0, waiting for transfers between devices: 247 us -> none
    ppermute x0 -> x48, waiting for transfers between devices: none -> 77.9 us  [swap(): return lax.ppermute(values, axis, [(i, i ^ bit) for i in range(size)])]
    psum x2 -> x0, blocking collectives: 52.2 us -> none  [the longest x1 40.9 us: local(): lax.psum((grad_self_query_bias, grad_self_value_bias, grad_self_out_bias,...]
    ppermute x0 -> x48, starting transfers between devices: none -> 45.8 us  [swap(): return lax.ppermute(values, axis, [(i, i ^ bit) for i in range(size)])]
    all_gather x5 -> x0, blocking collectives: 44.3 us -> none  [the longest x1 10.7 us: local(): lax.all_gather(self_keys, 'pb', axis=1, tiled=True)]
    dot_general x8 -> x2, matrix products: 41.4 us -> 7.76 us  [attend(): jnp.einsum('bhqk,bkhd->bqhd', low, value_rows, preferred_element_type=jnp...]
    dot_general x0 -> x12, local copies, waits for them, and re-layouts: none -> 22.5 us  [outer_sum(): jnp.einsum('bnd,bne->de', left, grad_rows, preferred_element_type=jnp.flo...]
  transfers between devices with their start and end apart: 26 -> 48, of which waited for: 22 -> 22; matrix products, arithmetic and copies ran while one was open for 9% -> 58% of each run, Pallas kernels for 0% -> 0%
where the time goes in v1:
time: 448 us; the launch traced here: 440 us
  local copies, waits for them, and re-layouts  146 us (33%)
  matrix products  97.3 us (22%)
  waiting for transfers between devices  77.9 us (17%)
  other arithmetic  70.6 us (16%)
  starting transfers between devices  45.8 us (10%)
    ppermute x48, waiting for transfers between devices, swap(): return lax.ppermute(values, axis, [(i, i ^ bit) for i in range(size)])  77.9 us
    ppermute x48, starting transfers between devices, swap(): return lax.ppermute(values, axis, [(i, i ^ bit) for i in range(size)])  45.8 us
    unnamed x236, local copies, waits for them, and re-layouts  31 us
    convert_element_type x4, local copies, waits for them, and re-layouts, reduce_blocks(): total = blocks.astype(jnp.bfloat16)  24.6 us
    dot_general x12, local copies, waits for them, and re-layouts, outer_sum(): jnp.einsum('bnd,bne->de', left, grad_rows, preferred_element_type=jnp.flo...  22.5 us
    dot_general x10, matrix products, back_linear(): jnp.einsum('bne,de->bnd', grad_rows, weight, preferred_element_type=jnp.f...  21.9 us
    dot_general x10, matrix products, linear(): return jnp.dot(left, right, preferred_element_type=jnp.float32)  19.7 us
    dynamic_slice x5, other arithmetic, pick(): return lax.dynamic_index_in_dim(values, index, axis, keepdims=False)  15.9 us
  transfers between devices with their start and end apart: 48, of which 22 were waited for; matrix products, arithmetic and copies ran while one was open for 58% of the time, Pallas kernels for 0%

profile of v1, /device:TPU:0, one launch (start us, length us, event | category | flops | bytes accessed | tf_op | source)
XLA Modules:
  0.0 440.5 jit_solution(17326850427108831722)
XLA Ops:
  0.7 2.5 collective-permute-start.5
  3.8 2.7 constant_dynamic-slice_fusion.14
  12.0 4.6 %fusion.29 = bf16[512,2,1208]{0,2,1:T(8,128)(2,1)} fusion(f32[1208,512]{1,0:T(8,128)} %constant.418.clone, bf16[8,1208,512]{2,1,0:T(8,128)(2,1)} %param.31, s32[]{:T(128)S(6)} %select_n.253), kind=kLoop, calls=%fused_computation.62 | loop fusion | flops 3710976 | bytes 7421956 | tf_op jit(solution)/shard_map/bnd,bne->de/dot_general | solution.py:37
  16.6 4.8 %convolution_convert_fusion.1 = bf16[2,1208,512]{2,1,0:T(8,128)(2,1)} fusion(f32[1208,512]{1,0:T(8,128)S(1)} %copy-done.3, bf16[8,1208,512]{2,1,0:T(8,128)(2,1)} %param.31, s32[]{:T(128)S(6)} %select_n.253, bf16[512,512]{1,0:T(8,128)(2,1)S(1)} %copy-done.36), kind=kOutput, calls=%fused_computation.21 | convolution fusion | flops 1271627776 | bytes 7946244 | tf_op jit(solution)/shard_map/dot_general | solution.py:29
  21.9 2.9 add_convert_fusion.2
  28.9 4.6 %copy.350 = bf16[2,1208,512]{1,2,0:T(8,128)(2,1)} copy(bf16[2,1208,512]{2,1,0:T(8,128)(2,1)} %add_convert_fusion.2) | data formatting | bytes 4947968 | tf_op jit(solution)/shard_map/convert_element_type | solution.py:211
  42.5 4.4 copy.352
  54.5 4.4 copy.406
  58.9 4.4 copy.403
  67.0 2.1 fusion.100
  69.0 1.8 copy.345
  70.8 2.1 fusion.101
  74.1 2.3 convolution_convert_fusion.6
  76.4 1.8 copy.347
  78.2 2.4 fusion.182
  80.6 1.8 convolution_convert_fusion.3
  84.9 1.9 fusion.172
  89.5 8.6 %fusion.184 = (f32[2,8,100]{2,1,0:T(8,128)}, f32[2,8,100,1208]{3,2,1,0:T(8,128)}) fusion(pred[2,1208]{1,0:T(4,128)(4,1)} %iota_compare_fusion, bf16[2,100,8,64]{1,3,2,0:T(8,128)(2,1)S(1)} %bitcast.539, bf16[2,1208,8,64]{1,3,2,0:T(8,128)(2,1)} %bitcast.516), kind=kOutput, calls=%fused_computation.373 | convolution fusion | flops 255130800 | bytes 10418800 | tf_op jit(solution)/shard_map/sub | solution.py:60
  98.2 6.0 %fusion.88 = bf16[2,8,64,100]{3,2,1,0:T(8,128)(2,1)S(1)} fusion(bf16[2,1208,8,64]{1,3,2,0:T(8,128)(2,1)} %bitcast.525, f32[2,8,100,1208]{3,2,1,0:T(8,128)} %get-tuple-element.117, f32[2,8,100]{2,1,0:T(8,128)} %get-tuple-element.116), kind=kOutput, calls=%fused_computation.123 | convolution fusion | flops 251366400 | bytes 10416384 | tf_op jit(solution)/shard_map/bhqk,bkhd->bqhd/dot_general | solution.py:63
  106.4 6.6 %multiply_convert_fusion.2 = (bf16[2,100,3200]{2,1,0:T(8,128)(2,1)S(1)}, f32[2,100,3200]{2,1,0:T(8,128)S(1)}) fusion(f32[2,100,3200]{2,1,0:T(8,128)S(1)} %get-tuple-element.120, u8[100,3200]{1,0:T(8,128)(4,1)S(1)} %get-tuple-element.29, u8[100,3200]{1,0:T(8,128)(4,1)S(1)} %get-tuple-element.28), kind=kLoop, calls=%fused_computation.43 | loop fusion | flops 44800000 | bytes 7040000 | tf_op jit(solution)/shard_map/convert_element_type | solution.py:242
  115.4 1.8 fusion.139
  117.2 2.4 convert_reduce_fusion.6
  119.7 2.4 convert_reduce_fusion.1
  122.1 3.1 multiply_reduce_fusion.2
  127.4 5.3 %multiply_reduce_fusion = (f32[2,8,100]{2,1,0:T(8,128)S(1)}, f32[2,8,100,1208]{3,2,1,0:T(8,128)S(1)}) fusion(f32[2,8,100,1208]{3,2,1,0:T(8,128)} %get-tuple-element.117, f32[2,8,100]{2,1,0:T(8,128)S(1)} %copy-done.91, bf16[2,100,8,64]{1,3,2,0:T(8,128)(2,1)} %bitcast.571, bf16[2,1208,8,64]{1,3,2,0:T(8,128)(2,1)S(1)} %bitcast.526), kind=kOutput, calls=%fused_computation.3 | convolution fusion | flops 253195200 | bytes 18153984 | tf_op jit(solution)/shard_map/bqhd,bkhd->bhqk/dot_general | solution.py:68
  135.1 2.2 convert_reduce_fusion.3
  137.4 1.8 multiply_reduce_fusion.3
  140.7 2.0 convert_reduce_fusion.4
  146.5 2.3 multiply_convert_fusion.1
  148.9 6.9 %convert_reduce_fusion = (f32[8,64]{1,0:T(8,128)}, bf16[2,8,64,1208]{3,2,1,0:T(8,128)(2,1)}) fusion(bf16[2,100,8,64]{1,3,2,0:T(8,128)(2,1)S(1)} %bitcast.572, f32[2,8,100,1208]{3,2,1,0:T(8,128)} %get-tuple-element.117, f32[2,8,100]{2,1,0:T(8,128)S(1)} %copy-done.91), kind=kOutput, calls=%fused_computation.10 | convolution fusion | flops 254974464 | bytes 10418432 | tf_op jit(solution)/shard_map/bhqk,bqhd->bkhd/dot_general | solution.py:81
  158.7 3.0 bitcast_convert_fusion.1
  165.3 1.8 copy.394
  168.0 2.5 add_reduce_fusion
  173.5 3.9 fusion.116
  180.7 3.1 rev.6
  185.6 1.8 convert_element_type.628
  196.1 2.1 fusion.81
  198.1 2.1 fusion.82
  238.3 9.5 %convert_element_type.696 = bf16[2,2,2,64,2,2,800]{6,5,4,3,2,1,0:T(2,128)(2,1)} reshape(bf16[512,3200]{1,0:T(8,128)(2,1)} %bitcast_convert_fusion.1) | data formatting | bytes 6553600 | tf_op jit(solution)/shard_map/convert_element_type | solution.py:113
  247.8 3.5 copy.413
  251.3 9.8 %convert_element_type.718 = bf16[2,2,800,2,2,2,64]{2,1,0,6,5,4,3:T(2,128)(2,1)} reshape(bf16[3200,512]{0,1:T(8,128)(2,1)} %copy.413) | data formatting | bytes 6553600 | tf_op jit(solution)/shard_map/convert_element_type | solution.py:113
  261.2 14.8 %constant_dynamic-slice_fusion.2 = (bf16[2,2,2,64,2,1,800]{6,5,4,3,2,1,0:T(2,128)(2,1)}, bf16[2,2,2,64,2,1,800]{6,5,4,3,2,1,0:T(2,128)(2,1)}) fusion(bf16[2,2,2,64,2,2,800]{6,5,4,3,2,1,0:T(2,128)(2,1)} %convert_element_type.696, s32[]{:T(128)S(6)} %select_n.269, s32[]{:T(128)S(6)} %select_n.270), kind=kLoop, calls=%fused_computation.290 | loop fusion | bytes 6553608 | tf_op jit(solution)/shard_map/jit(dynamic_index_in_dim)/dynamic_slice | solution.py:100
  276.0 13.9 %dynamic-slice_bitcast_fusion = (bf16[1,2,2,2,2,800,64]{5,0,2,6,1,3,4:T(2,128)(2,1)}, f32[1,2,2,2,2,800,64]{5,0,2,6,1,3,4:T(1,128)}) fusion(bf16[2,2,800,2,2,2,64]{2,1,0,6,5,4,3:T(2,128)(2,1)} %convert_element_type.718, s32[]{:T(128)S(6)} %select_n.270, s32[]{:T(128)S(6)} %select_n.269), kind=kLoop, calls=%fused_computation.27 | loop fusion | flops 819200 | bytes 8192008 | tf_op jit(solution)/shard_map/jit(dynamic_index_in_dim)/dynamic_slice | solution.py:100
  290.2 4.9 %add_convert_fusion = bf16[2,1208,512]{2,1,0:T(8,128)(2,1)S(1)} fusion(f32[2,1208,512]{2,1,0:T(8,128)} %fusion.116, bf16[2,1208,512]{1,2,0:T(8,128)(2,1)} %bitcast.521, bf16[512,512]{1,0:T(8,128)(2,1)S(1)} %copy-done.67), kind=kOutput, calls=%fused_computation.12 | convolution fusion | flops 1269153792 | bytes 10420224 | tf_op jit(solution)/shard_map/bne,de->bnd/dot_general | solution.py:33
  301.4 1.9 copy.415
  317.1 8.8 %collective-permute-done.20 = bf16[2,2,25,64]{3,0,1,2:T(2,128)(2,1)S(1)} collective-permute-done((bf16[2,2,25,64]{3,0,1,2:T(2,128)(2,1)S(1)}, bf16[2,2,25,64]{3,0,1,2:T(2,128)(2,1)S(1)}, u32[]{:S(2)}, u32[]{:S(2)}) %collective-permute-start.20) | collective-permute-done | bytes 12832 | tf_op jit(solution)/shard_map/ppermute | solution.py:96
  327.5 2.4 collective-permute-done.29
  335.0 2.5 collective-permute-done.30
  337.6 2.6 collective-permute-start.22
  341.9 2.3 collective-permute-done.31
  345.3 3.9 collective-permute-done.32
  357.0 8.5 %collective-permute-done.17 = bf16[2,302,512]{2,0,1:T(2,128)(2,1)S(1)} collective-permute-done((bf16[2,302,512]{2,0,1:T(2,128)(2,1)S(1)}, bf16[2,302,512]{2,0,1:T(2,128)(2,1)S(1)}, u32[]{:S(2)}, u32[]{:S(2)}) %collective-permute-start.17) | collective-permute-done | bytes 618528 | tf_op jit(solution)/shard_map/ppermute | solution.py:96
  366.3 2.0 collective-permute-done.24
  369.2 10.0 %collective-permute-done.34 = bf16[2,2,2,4,64,128]{5,4,0,1,2,3:T(8,128)(2,1)S(1)} collective-permute-done((bf16[2,2,2,4,64,128]{5,4,0,1,2,3:T(8,128)(2,1)S(1)}, bf16[2,2,2,4,64,128]{5,4,0,1,2,3:T(8,128)(2,1)S(1)}, u32[]{:S(2)}, u32[]{:S(2)}) %collective-permute-start.34) | collective-permute-done | bytes 524320 | tf_op jit(solution)/shard_map/ppermute | solution.py:96
  382.2 2.5 fusion.6
  390.4 2.7 collective-permute-done.26
  396.3 2.4 collective-permute-done.27
  400.6 6.5 %collective-permute-done.39 = bf16[2,2,2,64,800]{4,3,2,1,0:T(8,128)(2,1)S(1)} collective-permute-done((bf16[2,2,2,64,800]{4,3,2,1,0:T(8,128)(2,1)S(1)}, bf16[2,2,2,64,800]{4,3,2,1,0:T(8,128)(2,1)S(1)}, u32[]{:S(2)}, u32[]{:S(2)}) %collective-permute-start.39) | collective-permute-done | bytes 819232 | tf_op jit(solution)/shard_map/ppermute | solution.py:96
  410.1 1.7 constant_dynamic-slice_fusion
  413.3 5.5 %collective-permute-done.40 = bf16[2,2,64,800]{3,2,1,0:T(8,128)(2,1)S(1)} collective-permute-done((bf16[2,2,64,800]{3,2,1,0:T(8,128)(2,1)S(1)}, bf16[2,2,64,800]{3,2,1,0:T(8,128)(2,1)S(1)}, u32[]{:S(2)}, u32[]{:S(2)}) %collective-permute-start.40) | collective-permute-done | bytes 409632 | tf_op jit(solution)/shard_map/ppermute | solution.py:96
  420.5 2.4 collective-permute-done.45
  424.8 3.0 collective-permute-done.41
  428.2 2.9 collective-permute-done.46
  431.9 6.3 %collective-permute-done.42 = bf16[64,800]{1,0:T(8,128)(2,1)S(1)} collective-permute-done((bf16[64,800]{1,0:T(8,128)(2,1)S(1)}, bf16[64,800]{1,0:T(8,128)(2,1)S(1)}, u32[]{:S(2)}, u32[]{:S(2)}) %collective-permute-start.42) | collective-permute-done | bytes 102432 | tf_op jit(solution)/shard_map/ppermute | solution.py:96
  (481 shorter events, 177.6 us)
Async XLA Ops:
  0.7 104.2 %copy-start = (bf16[512,3200]{1,0:T(8,128)(2,1)S(1)}, bf16[512,3200]{1,0:T(8,128)(2,1)}, u32[]{:S(2)}) copy-start(bf16[512,3200]{1,0:T(8,128)(2,1)} %param.52) | copy-start | bytes 9830404
  0.7 62.5 %collective-permute-start.5 = (bf16[25,512]{1,0:T(8,128)(2,1)}, bf16[25,512]{1,0:T(8,128)(2,1)}, u32[]{:S(2)}, u32[]{:S(2)}) collective-permute-start(bf16[25,512]{1,0:T(8,128)(2,1)} %param.33), channel_id=1, source_target_pairs={{0,3},{1,2},{2,1},{3,0},{4,7},{5,6},{6,5},{7,4},{8,11},{9,10},{10,... | collective-permute-start | bytes 76808 | tf_op jit(solution)/shard_map/ppermute | solution.py:96
  3.2 60.1 %collective-permute-start.4 = (bf16[25,512]{1,0:T(8,128)(2,1)}, bf16[25,512]{1,0:T(8,128)(2,1)}, u32[]{:S(2)}, u32[]{:S(2)}) collective-permute-start(bf16[25,512]{1,0:T(8,128)(2,1)} %param.33), channel_id=1, source_target_pairs={{0,2},{1,3},{2,0},{3,1},{4,6},{5,7},{6,4},{7,5},{8,10},{9,11},{10,... | collective-permute-start | bytes 76808 | tf_op jit(solution)/shard_map/ppermute | solution.py:96
  3.8 60.9 %collective-permute-start.3 = (bf16[25,512]{1,0:T(8,128)(2,1)}, bf16[25,512]{1,0:T(8,128)(2,1)}, u32[]{:S(2)}, u32[]{:S(2)}) collective-permute-start(bf16[25,512]{1,0:T(8,128)(2,1)} %param.33), channel_id=1, source_target_pairs={{0,1},{1,0},{2,3},{3,2},{4,5},{5,4},{6,7},{7,6},{8,9},{9,8},{10,11... | collective-permute-start | bytes 76808 | tf_op jit(solution)/shard_map/ppermute | solution.py:96
  7.1 59.1 %collective-permute-start.2 = (bf16[2,25,512]{2,1,0:T(8,128)(2,1)}, bf16[2,25,512]{2,1,0:T(8,128)(2,1)}, u32[]{:S(2)}, u32[]{:S(2)}) collective-permute-start(bf16[2,25,512]{2,1,0:T(8,128)(2,1)} %copy.496), channel_id=1, source_target_pairs={{0,3},{1,2},{2,1},{3,0},{4,7},{5,6},{6,5},{7,4},{8,11},{9,10},{10,... | collective-permute-start | bytes 153608 | tf_op jit(solution)/shard_map/ppermute | solution.py:96
  9.2 57.1 %collective-permute-start.1 = (bf16[2,25,512]{2,1,0:T(8,128)(2,1)}, bf16[2,25,512]{2,1,0:T(8,128)(2,1)}, u32[]{:S(2)}, u32[]{:S(2)}) collective-permute-start(bf16[2,25,512]{2,1,0:T(8,128)(2,1)} %copy.495), channel_id=1, source_target_pairs={{0,2},{1,3},{2,0},{3,1},{4,6},{5,7},{6,4},{7,5},{8,10},{9,11},{10,... | collective-permute-start | bytes 153608 | tf_op jit(solution)/shard_map/ppermute | solution.py:96
  35.0 35.9 %copy-start.56 = (bf16[2,25,512]{2,1,0:T(8,128)(2,1)}, bf16[2,25,512]{2,1,0:T(8,128)(2,1)S(1)}, u32[]{:S(2)}) copy-start(bf16[2,25,512]{2,1,0:T(8,128)(2,1)S(1)} %copy.493) | copy-start | bytes 153604
  63.2 3.1 collective-permute-start
  63.2 50.9 %collective-permute-start.11 = (bf16[2,25,512]{2,1,0:T(8,128)(2,1)}, bf16[2,25,512]{2,1,0:T(8,128)(2,1)}, u32[]{:S(2)}, u32[]{:S(2)}) collective-permute-start(bf16[2,25,512]{2,1,0:T(8,128)(2,1)} %copy.500), channel_id=1, source_target_pairs={{0,3},{1,2},{2,1},{3,0},{4,7},{5,6},{6,5},{7,4},{8,11},{9,10},{10,... | collective-permute-start | bytes 153608 | tf_op jit(solution)/shard_map/ppermute | solution.py:96
  64.7 49.5 %collective-permute-start.10 = (bf16[2,25,512]{2,1,0:T(8,128)(2,1)}, bf16[2,25,512]{2,1,0:T(8,128)(2,1)}, u32[]{:S(2)}, u32[]{:S(2)}) collective-permute-start(bf16[2,25,512]{2,1,0:T(8,128)(2,1)} %copy.499), channel_id=1, source_target_pairs={{0,2},{1,3},{2,0},{3,1},{4,6},{5,7},{6,4},{7,5},{8,10},{9,11},{10,... | collective-permute-start | bytes 153608 | tf_op jit(solution)/shard_map/ppermute | solution.py:96
  66.2 47.9 %collective-permute-start.9 = (bf16[2,25,512]{2,1,0:T(8,128)(2,1)}, bf16[2,25,512]{2,1,0:T(8,128)(2,1)}, u32[]{:S(2)}, u32[]{:S(2)}) collective-permute-start(bf16[2,25,512]{2,1,0:T(8,128)(2,1)} %copy.498), channel_id=1, source_target_pairs={{0,1},{1,0},{2,3},{3,2},{4,5},{5,4},{6,7},{7,6},{8,9},{9,8},{10,11... | collective-permute-start | bytes 153608 | tf_op jit(solution)/shard_map/ppermute | solution.py:96
  104.6 20.6 %copy-start.16 = (f32[2,100,512]{2,1,0:T(8,128)}, f32[2,100,512]{2,1,0:T(8,128)S(1)}, u32[]{:S(2)}) copy-start(f32[2,100,512]{2,1,0:T(8,128)S(1)} %get-tuple-element.119) | copy-start | bytes 1228804
  163.4 142.9 %collective-permute-start.6 = (bf16[2,25,512]{2,1,0:T(8,128)(2,1)}, bf16[2,25,512]{2,1,0:T(8,128)(2,1)}, u32[]{:S(2)}, u32[]{:S(2)}) collective-permute-start(bf16[2,25,512]{2,1,0:T(8,128)(2,1)} %get-tuple-element.73), channel_id=1, source_target_pairs={{0,1},{1,0},{2,3},{3,2},{4,5},{5,4},{6,7},{7,6},{8,9},{9,8},{10,11... | collective-permute-start | bytes 153608 | tf_op jit(solution)/shard_map/ppermute | solution.py:96
  163.9 143.7 %collective-permute-start.7 = (bf16[2,25,512]{2,1,0:T(8,128)(2,1)}, bf16[2,25,512]{2,1,0:T(8,128)(2,1)}, u32[]{:S(2)}, u32[]{:S(2)}) collective-permute-start(bf16[2,25,512]{2,1,0:T(8,128)(2,1)} %get-tuple-element.72), channel_id=1, source_target_pairs={{0,2},{1,3},{2,0},{3,1},{4,6},{5,7},{6,4},{7,5},{8,10},{9,11},{10,... | collective-permute-start | bytes 153608 | tf_op jit(solution)/shard_map/ppermute | solution.py:96
  165.3 144.0 %collective-permute-start.8 = (bf16[2,25,512]{2,1,0:T(8,128)(2,1)}, bf16[2,25,512]{2,1,0:T(8,128)(2,1)}, u32[]{:S(2)}, u32[]{:S(2)}) collective-permute-start(bf16[2,25,512]{2,1,0:T(8,128)(2,1)} %get-tuple-element.71), channel_id=1, source_target_pairs={{0,3},{1,2},{2,1},{3,0},{4,7},{5,6},{6,5},{7,4},{8,11},{9,10},{10,... | collective-permute-start | bytes 153608 | tf_op jit(solution)/shard_map/ppermute | solution.py:96
  172.8 139.2 %collective-permute-start.12 = (bf16[2,25,512]{2,1,0:T(8,128)(2,1)}, bf16[2,25,512]{2,1,0:T(8,128)(2,1)}, u32[]{:S(2)}, u32[]{:S(2)}) collective-permute-start(bf16[2,25,512]{2,1,0:T(8,128)(2,1)} %get-tuple-element.69), channel_id=1, source_target_pairs={{0,1},{1,0},{2,3},{3,2},{4,5},{5,4},{6,7},{7,6},{8,9},{9,8},{10,11... | collective-permute-start | bytes 153608 | tf_op jit(solution)/shard_map/ppermute | solution.py:96
  173.5 14.5 %copy-start.57 = (bf16[2,25,512]{2,1,0:T(8,128)(2,1)S(1)}, bf16[2,25,512]{2,1,0:T(8,128)(2,1)}, u32[]{:S(2)}) copy-start(bf16[2,25,512]{2,1,0:T(8,128)(2,1)} %copy-done.56) | copy-start | bytes 153604
  189.1 28.4 %copy-start.93 = (f32[512]{0:T(512)S(1)}, f32[512]{0:T(512)}, u32[]{:S(2)}) copy-start(f32[512]{0:T(512)} %get-tuple-element.34) | copy-start | bytes 6148
  189.1 29.7 %copy-start.92 = (f32[512]{0:T(512)S(1)}, f32[512]{0:T(512)}, u32[]{:S(2)}) copy-start(f32[512]{0:T(512)} %get-tuple-element.40) | copy-start | bytes 6148
  220.1 83.3 %collective-permute-start.28 = (f32[77,128]{1,0:T(8,128)}, f32[77,128]{1,0:T(8,128)}, u32[]{:S(2)}, u32[]{:S(2)}) collective-permute-start(f32[77,128]{1,0:T(8,128)} %bitcast.575), channel_id=1, source_target_pairs={{0,1},{1,0},{2,3},{3,2},{4,5},{5,4},{6,7},{7,6},{8,9},{9,8},{10,11... | collective-permute-start | bytes 118280 | tf_op jit(solution)/shard_map/ppermute | solution.py:96
  276.0 13.9 %copy-start.72 = (bf16[2,25,512]{2,1,0:T(8,128)(2,1)S(1)}, bf16[2,25,512]{2,1,0:T(8,128)(2,1)}, u32[]{:S(2)}) copy-start(bf16[2,25,512]{2,1,0:T(8,128)(2,1)} %get-tuple-element.74) | copy-start | bytes 153604
  276.0 14.0 %copy-start.73 = (bf16[2,25,512]{2,1,0:T(8,128)(2,1)S(1)}, bf16[2,25,512]{2,1,0:T(8,128)(2,1)}, u32[]{:S(2)}) copy-start(bf16[2,25,512]{2,1,0:T(8,128)(2,1)} %get-tuple-element.70) | copy-start | bytes 153604
  276.0 14.1 %copy-start.67 = (bf16[512,512]{1,0:T(8,128)(2,1)S(1)}, bf16[512,512]{1,0:T(8,128)(2,1)}, u32[]{:S(2)}) copy-start(bf16[512,512]{1,0:T(8,128)(2,1)} %param.46) | copy-start | bytes 1572868
  301.4 14.8 %copy-start.47 = (bf16[2,2,2,2,4,64,128]{6,5,1,0,2,3,4:T(8,128)(2,1)S(1)}, bf16[2,2,2,2,4,64,128]{6,5,1,0,2,3,4:T(8,128)(2,1)}, u32[]{:S(2)}) copy-start(bf16[2,2,2,2,4,64,128]{6,5,1,0,2,3,4:T(8,128)(2,1)} %dynamic-slice_bitcast_fusion.3) | copy-start | bytes 3145732
  301.4 42.8 %copy-start.48 = (bf16[2,2,2,2,4,64,128]{6,5,1,0,2,3,4:T(8,128)(2,1)S(1)}, bf16[2,2,2,2,4,64,128]{6,5,1,0,2,3,4:T(8,128)(2,1)}, u32[]{:S(2)}) copy-start(bf16[2,2,2,2,4,64,128]{6,5,1,0,2,3,4:T(8,128)(2,1)} %dynamic-slice_bitcast_fusion.2) | copy-start | bytes 3145732
  303.3 49.6 %copy-start.19 = (bf16[2,2,2,2,2,4,64,128]{7,6,0,2,1,3,4,5:T(8,128)(2,1)S(1)}, bf16[2,2,2,2,2,4,64,128]{7,6,0,2,1,3,4,5:T(8,128)(2,1)}, u32[]{:S(2)}) copy-start(bf16[2,2,2,2,2,4,64,128]{7,6,0,2,1,3,4,5:T(8,128)(2,1)} %copy-done.18) | copy-start | bytes 6291460
  303.3 1.5 collective-permute-start.18
  304.8 11.5 %collective-permute-start.13 = (bf16[2,25,512]{2,1,0:T(8,128)(2,1)S(1)}, bf16[2,25,512]{2,1,0:T(8,128)(2,1)S(1)}, u32[]{:S(2)}, u32[]{:S(2)}) collective-permute-start(bf16[2,25,512]{2,1,0:T(8,128)(2,1)S(1)} %copy-done.79), channel_id=1, source_target_pairs={{0,2},{1,3},{2,0},{3,1},{4,6},{5,7},{6,4},{7,5},{8,10},{9,11},{10,... | collective-permute-start | bytes 153608 | tf_op jit(solution)/shard_map/ppermute | solution.py:96
  306.4 33.8 %collective-permute-start.14 = (bf16[2,25,512]{2,1,0:T(8,128)(2,1)S(1)}, bf16[2,25,512]{2,1,0:T(8,128)(2,1)S(1)}, u32[]{:S(2)}, u32[]{:S(2)}) collective-permute-start(bf16[2,25,512]{2,1,0:T(8,128)(2,1)S(1)} %copy-done.78), channel_id=1, source_target_pairs={{0,3},{1,2},{2,1},{3,0},{4,7},{5,6},{6,5},{7,4},{8,11},{9,10},{10,... | collective-permute-start | bytes 153608 | tf_op jit(solution)/shard_map/ppermute | solution.py:96
  307.7 43.2 %collective-permute-start.15 = (bf16[2,302,512]{2,0,1:T(2,128)(2,1)S(1)}, bf16[2,302,512]{2,0,1:T(2,128)(2,1)S(1)}, u32[]{:S(2)}, u32[]{:S(2)}) collective-permute-start(bf16[2,302,512]{2,0,1:T(2,128)(2,1)S(1)} %copy.378), channel_id=1, source_target_pairs={{0,1},{1,0},{2,3},{3,2},{4,5},{5,4},{6,7},{7,6},{8,9},{9,8},{10,11... | collective-permute-start | bytes 1855496 | tf_op jit(solution)/shard_map/ppermute | solution.py:96
  309.3 46.1 %collective-permute-start.16 = (bf16[2,302,512]{2,0,1:T(2,128)(2,1)S(1)}, bf16[2,302,512]{2,0,1:T(2,128)(2,1)S(1)}, u32[]{:S(2)}, u32[]{:S(2)}) collective-permute-start(bf16[2,302,512]{2,0,1:T(2,128)(2,1)S(1)} %copy.379), channel_id=1, source_target_pairs={{0,2},{1,3},{2,0},{3,1},{4,6},{5,7},{6,4},{7,5},{8,10},{9,11},{10,... | collective-permute-start | bytes 1855496 | tf_op jit(solution)/shard_map/ppermute | solution.py:96
  311.7 41.7 %copy-start.74 = (bf16[8,25,512]{2,0,1:T(8,128)(2,1)}, bf16[8,25,512]{2,0,1:T(8,128)(2,1)S(1)}, u32[]{:S(2)}) copy-start(bf16[8,25,512]{2,0,1:T(8,128)(2,1)S(1)} %copy_dynamic-update-slice_fusion.5) | copy-start | bytes 614404
  312.0 4.2 collective-permute-start.19
  316.2 36.7 %collective-permute-start.23 = (bf16[2,2,2,2,4,64,128]{6,5,1,0,2,3,4:T(8,128)(2,1)S(1)}, bf16[2,2,2,2,4,64,128]{6,5,1,0,2,3,4:T(8,128)(2,1)S(1)}, u32[]{:S(2)}, u32[]{:S(2)}) collective-permute-start(bf16[2,2,2,2,4,64,128]{6,5,1,0,2,3,4:T(8,128)(2,1)S(1)} %copy-done.47), channel_id=1, source_target_pairs={{0,1},{1,0},{2,3},{3,2},{4,5},{5,4},{6,7},{7,6},{8,9},{9,8},{10,11... | collective-permute-start | bytes 3145736 | tf_op jit(solution)/shard_map/ppermute | solution.py:96
  316.3 9.6 %collective-permute-start.20 = (bf16[2,2,25,64]{3,0,1,2:T(2,128)(2,1)S(1)}, bf16[2,2,25,64]{3,0,1,2:T(2,128)(2,1)S(1)}, u32[]{:S(2)}, u32[]{:S(2)}) collective-permute-start(bf16[2,2,25,64]{3,0,1,2:T(2,128)(2,1)S(1)} %dynamic-slice_bitcast_fusion.20), channel_id=1, source_target_pairs={{0,2},{1,3},{2,0},{3,1},{4,6},{5,7},{6,4},{7,5},{8,10},{9,11},{10,... | collective-permute-start | bytes 38408 | tf_op jit(solution)/shard_map/ppermute | solution.py:96
  325.9 4.0 collective-permute-start.29
  329.9 3.7 collective-permute-start.21
  333.6 4.0 collective-permute-start.30
  337.6 6.7 %collective-permute-start.22 = (bf16[25,64]{1,0:T(8,128)(2,1)S(1)}, bf16[25,64]{1,0:T(8,128)(2,1)S(1)}, u32[]{:S(2)}, u32[]{:S(2)}) collective-permute-start(bf16[25,64]{1,0:T(8,128)(2,1)S(1)} %bitcast.579), channel_id=1, source_target_pairs={{0,16},{4,20},{8,24},{12,28},{16,0},{20,4},{24,8},{28,12},{1,17},{... | collective-permute-start | bytes 9608 | tf_op jit(solution)/shard_map/ppermute | solution.py:96
  340.2 4.1 collective-permute-start.31
  344.2 9.2 %collective-permute-start.33 = (bf16[2,2,2,2,4,64,128]{6,5,1,0,2,3,4:T(8,128)(2,1)S(1)}, bf16[2,2,2,2,4,64,128]{6,5,1,0,2,3,4:T(8,128)(2,1)S(1)}, u32[]{:S(2)}, u32[]{:S(2)}) collective-permute-start(bf16[2,2,2,2,4,64,128]{6,5,1,0,2,3,4:T(8,128)(2,1)S(1)} %copy-done.48), channel_id=1, source_target_pairs={{0,1},{1,0},{2,3},{3,2},{4,5},{5,4},{6,7},{7,6},{8,9},{9,8},{10,11... | collective-permute-start | bytes 3145736 | tf_op jit(solution)/shard_map/ppermute | solution.py:96
  344.3 5.0 %collective-permute-start.32 = (f32[77,128]{1,0:T(8,128)S(1)}, f32[77,128]{1,0:T(8,128)S(1)}, u32[]{:S(2)}, u32[]{:S(2)}) collective-permute-start(f32[77,128]{1,0:T(8,128)S(1)} %add.516), channel_id=1, source_target_pairs={{0,16},{4,20},{8,24},{12,28},{16,0},{20,4},{24,8},{28,12},{1,17},{... | collective-permute-start | bytes 118280 | tf_op jit(solution)/shard_map/ppermute | solution.py:96
  349.2 16.2 %collective-permute-start.17 = (bf16[2,302,512]{2,0,1:T(2,128)(2,1)S(1)}, bf16[2,302,512]{2,0,1:T(2,128)(2,1)S(1)}, u32[]{:S(2)}, u32[]{:S(2)}) collective-permute-start(bf16[2,302,512]{2,0,1:T(2,128)(2,1)S(1)} %copy.380), channel_id=1, source_target_pairs={{0,3},{1,2},{2,1},{3,0},{4,7},{5,6},{6,5},{7,4},{8,11},{9,10},{10,... | collective-permute-start | bytes 1855496 | tf_op jit(solution)/shard_map/ppermute | solution.py:96
  350.8 29.2 %collective-permute-start.38 = (bf16[2,2,2,2,64,800]{5,4,3,2,1,0:T(8,128)(2,1)S(1)}, bf16[2,2,2,2,64,800]{5,4,3,2,1,0:T(8,128)(2,1)S(1)}, u32[]{:S(2)}, u32[]{:S(2)}) collective-permute-start(bf16[2,2,2,2,64,800]{5,4,3,2,1,0:T(8,128)(2,1)S(1)} %bitcast.538), channel_id=1, source_target_pairs={{0,1},{1,0},{2,3},{3,2},{4,5},{5,4},{6,7},{7,6},{8,9},{9,8},{10,11... | collective-permute-start | bytes 4915208 | tf_op jit(solution)/shard_map/ppermute | solution.py:96
  352.9 29.3 %collective-permute-start.43 = (bf16[2,2,2,2,800,64]{4,1,5,0,2,3:T(2,128)(2,1)S(1)}, bf16[2,2,2,2,800,64]{4,1,5,0,2,3:T(2,128)(2,1)S(1)}, u32[]{:S(2)}, u32[]{:S(2)}) collective-permute-start(bf16[2,2,2,2,800,64]{4,1,5,0,2,3:T(2,128)(2,1)S(1)} %copy.415), channel_id=1, source_target_pairs={{0,1},{1,0},{2,3},{3,2},{4,5},{5,4},{6,7},{7,6},{8,9},{9,8},{10,11... | collective-permute-start | bytes 4915208 | tf_op jit(solution)/shard_map/ppermute | solution.py:96
  353.5 14.8 %collective-permute-start.24 = (bf16[2,2,2,4,64,128]{5,4,0,1,2,3:T(8,128)(2,1)S(1)}, bf16[2,2,2,4,64,128]{5,4,0,1,2,3:T(8,128)(2,1)S(1)}, u32[]{:S(2)}, u32[]{:S(2)}) collective-permute-start(bf16[2,2,2,4,64,128]{5,4,0,1,2,3:T(8,128)(2,1)S(1)} %dynamic-slice_bitcast_fusion.7), channel_id=1, source_target_pairs={{0,4},{4,0},{8,12},{12,8},{16,20},{20,16},{24,28},{28,24},{1,5},{5... | collective-permute-start | bytes 1572872 | tf_op jit(solution)/shard_map/ppermute | solution.py:96
  355.5 23.7 %collective-permute-start.34 = (bf16[2,2,2,4,64,128]{5,4,0,1,2,3:T(8,128)(2,1)S(1)}, bf16[2,2,2,4,64,128]{5,4,0,1,2,3:T(8,128)(2,1)S(1)}, u32[]{:S(2)}, u32[]{:S(2)}) collective-permute-start(bf16[2,2,2,4,64,128]{5,4,0,1,2,3:T(8,128)(2,1)S(1)} %dynamic-slice_bitcast_fusion.6), channel_id=1, source_target_pairs={{0,4},{4,0},{8,12},{12,8},{16,20},{20,16},{24,28},{28,24},{1,5},{5... | collective-permute-start | bytes 1572872 | tf_op jit(solution)/shard_map/ppermute | solution.py:96
  357.0 23.1 %copy-start.8 = (bf16[2,2,2,64,2,1,800]{6,5,4,3,2,1,0:T(2,128)(2,1)S(1)}, bf16[2,2,2,64,2,1,800]{6,5,4,3,2,1,0:T(2,128)(2,1)}, u32[]{:S(2)}) copy-start(bf16[2,2,2,64,2,1,800]{6,5,4,3,2,1,0:T(2,128)(2,1)} %get-tuple-element.56) | copy-start | bytes 4915204
  366.3 14.3 %copy-start.28 = (bf16[8,302,512]{2,0,1:T(8,128)(2,1)}, bf16[8,302,512]{2,0,1:T(8,128)(2,1)S(1)}, u32[]{:S(2)}) copy-start(bf16[8,302,512]{2,0,1:T(8,128)(2,1)S(1)} %constant_dynamic-update-slice_fusion) | copy-start | bytes 7421956
  368.5 18.4 %collective-permute-start.25 = (bf16[2,2,4,64,128]{4,3,0,1,2:T(8,128)(2,1)S(1)}, bf16[2,2,4,64,128]{4,3,0,1,2:T(8,128)(2,1)S(1)}, u32[]{:S(2)}, u32[]{:S(2)}) collective-permute-start(bf16[2,2,4,64,128]{4,3,0,1,2:T(8,128)(2,1)S(1)} %dynamic-slice_bitcast_fusion.10), channel_id=1, source_target_pairs={{0,2},{1,3},{2,0},{3,1},{4,6},{5,7},{6,4},{7,5},{8,10},{9,11},{10,... | collective-permute-start | bytes 786440 | tf_op jit(solution)/shard_map/ppermute | solution.py:96
  379.4 9.3 %collective-permute-start.35 = (bf16[2,2,4,64,128]{4,3,0,1,2:T(8,128)(2,1)S(1)}, bf16[2,2,4,64,128]{4,3,0,1,2:T(8,128)(2,1)S(1)}, u32[]{:S(2)}, u32[]{:S(2)}) collective-permute-start(bf16[2,2,4,64,128]{4,3,0,1,2:T(8,128)(2,1)S(1)} %dynamic-slice_bitcast_fusion.9), channel_id=1, source_target_pairs={{0,2},{1,3},{2,0},{3,1},{4,6},{5,7},{6,4},{7,5},{8,10},{9,11},{10,... | collective-permute-start | bytes 786440 | tf_op jit(solution)/shard_map/ppermute | solution.py:96
  380.7 26.3 %collective-permute-start.39 = (bf16[2,2,2,64,800]{4,3,2,1,0:T(8,128)(2,1)S(1)}, bf16[2,2,2,64,800]{4,3,2,1,0:T(8,128)(2,1)S(1)}, u32[]{:S(2)}, u32[]{:S(2)}) collective-permute-start(bf16[2,2,2,64,800]{4,3,2,1,0:T(8,128)(2,1)S(1)} %dynamic-slice_bitcast_fusion.5), channel_id=1, source_target_pairs={{0,2},{1,3},{2,0},{3,1},{4,6},{5,7},{6,4},{7,5},{8,10},{9,11},{10,... | collective-permute-start | bytes 2457608 | tf_op jit(solution)/shard_map/ppermute | solution.py:96
  385.4 23.5 %collective-permute-start.44 = (bf16[2,2,2,800,64]{3,0,4,1,2:T(2,128)(2,1)S(1)}, bf16[2,2,2,800,64]{3,0,4,1,2:T(2,128)(2,1)S(1)}, u32[]{:S(2)}, u32[]{:S(2)}) collective-permute-start(bf16[2,2,2,800,64]{3,0,4,1,2:T(2,128)(2,1)S(1)} %dynamic-slice_bitcast_fusion.4), channel_id=1, source_target_pairs={{0,4},{4,0},{8,12},{12,8},{16,20},{20,16},{24,28},{28,24},{1,5},{5... | collective-permute-start | bytes 2457608 | tf_op jit(solution)/shard_map/ppermute | solution.py:96
  387.0 6.1 %collective-permute-start.26 = (bf16[2,4,64,128]{3,2,0,1:T(8,128)(2,1)S(1)}, bf16[2,4,64,128]{3,2,0,1:T(8,128)(2,1)S(1)}, u32[]{:S(2)}, u32[]{:S(2)}) collective-permute-start(bf16[2,4,64,128]{3,2,0,1:T(8,128)(2,1)S(1)} %dynamic-slice_bitcast_fusion.14), channel_id=1, source_target_pairs={{0,8},{4,12},{8,0},{12,4},{16,24},{20,28},{24,16},{28,20},{1,9},{5... | collective-permute-start | bytes 393224 | tf_op jit(solution)/shard_map/ppermute | solution.py:96
  388.8 6.4 %collective-permute-start.36 = (bf16[2,4,64,128]{3,2,0,1:T(8,128)(2,1)S(1)}, bf16[2,4,64,128]{3,2,0,1:T(8,128)(2,1)S(1)}, u32[]{:S(2)}, u32[]{:S(2)}) collective-permute-start(bf16[2,4,64,128]{3,2,0,1:T(8,128)(2,1)S(1)} %dynamic-slice_bitcast_fusion.13), channel_id=1, source_target_pairs={{0,8},{4,12},{8,0},{12,4},{16,24},{20,28},{24,16},{28,20},{1,9},{5... | collective-permute-start | bytes 393224 | tf_op jit(solution)/shard_map/ppermute | solution.py:96
  393.2 5.5 %collective-permute-start.27 = (bf16[4,64,128]{2,1,0:T(8,128)(2,1)S(1)}, bf16[4,64,128]{2,1,0:T(8,128)(2,1)S(1)}, u32[]{:S(2)}, u32[]{:S(2)}) collective-permute-start(bf16[4,64,128]{2,1,0:T(8,128)(2,1)S(1)} %dynamic-slice_bitcast_fusion.19), channel_id=1, source_target_pairs={{0,16},{4,20},{8,24},{12,28},{16,0},{20,4},{24,8},{28,12},{1,17},{... | collective-permute-start | bytes 196616 | tf_op jit(solution)/shard_map/ppermute | solution.py:96
  395.3 5.3 %collective-permute-start.37 = (bf16[4,64,128]{2,1,0:T(8,128)(2,1)S(1)}, bf16[4,64,128]{2,1,0:T(8,128)(2,1)S(1)}, u32[]{:S(2)}, u32[]{:S(2)}) collective-permute-start(bf16[4,64,128]{2,1,0:T(8,128)(2,1)S(1)} %dynamic-slice_bitcast_fusion.18), channel_id=1, source_target_pairs={{0,16},{4,20},{8,24},{12,28},{16,0},{20,4},{24,8},{28,12},{1,17},{... | collective-permute-start | bytes 196616 | tf_op jit(solution)/shard_map/ppermute | solution.py:96
  407.4 11.4 %collective-permute-start.40 = (bf16[2,2,64,800]{3,2,1,0:T(8,128)(2,1)S(1)}, bf16[2,2,64,800]{3,2,1,0:T(8,128)(2,1)S(1)}, u32[]{:S(2)}, u32[]{:S(2)}) collective-permute-start(bf16[2,2,64,800]{3,2,1,0:T(8,128)(2,1)S(1)} %dynamic-slice_bitcast_fusion.8), channel_id=1, source_target_pairs={{0,4},{4,0},{8,12},{12,8},{16,20},{20,16},{24,28},{28,24},{1,5},{5... | collective-permute-start | bytes 1228808 | tf_op jit(solution)/shard_map/ppermute | solution.py:96
  411.9 11.1 %collective-permute-start.45 = (bf16[2,2,800,64]{2,3,0,1:T(8,128)(2,1)S(1)}, bf16[2,2,800,64]{2,3,0,1:T(8,128)(2,1)S(1)}, u32[]{:S(2)}, u32[]{:S(2)}) collective-permute-start(bf16[2,2,800,64]{2,3,0,1:T(8,128)(2,1)S(1)} %bitcast.567), channel_id=1, source_target_pairs={{0,2},{1,3},{2,0},{3,1},{4,6},{5,7},{6,4},{7,5},{8,10},{9,11},{10,... | collective-permute-start | bytes 1228808 | tf_op jit(solution)/shard_map/ppermute | solution.py:96
  418.7 21.5 %copy-start.1 = (bf16[512,3200]{1,0:T(8,128)(2,1)S(1)}, bf16[512,3200]{1,0:T(8,128)(2,1)}, u32[]{:S(2)}) copy-start(bf16[512,3200]{1,0:T(8,128)(2,1)} %param.52) | copy-start | bytes 9830404
  418.9 8.9 %collective-permute-start.41 = (bf16[2,64,800]{2,1,0:T(8,128)(2,1)S(1)}, bf16[2,64,800]{2,1,0:T(8,128)(2,1)S(1)}, u32[]{:S(2)}, u32[]{:S(2)}) collective-permute-start(bf16[2,64,800]{2,1,0:T(8,128)(2,1)S(1)} %dynamic-slice_bitcast_fusion.12), channel_id=1, source_target_pairs={{0,8},{4,12},{8,0},{12,4},{16,24},{20,28},{24,16},{28,20},{1,9},{5... | collective-permute-start | bytes 614408 | tf_op jit(solution)/shard_map/ppermute | solution.py:96
  423.1 8.0 %collective-permute-start.46 = (bf16[2,800,64]{1,2,0:T(8,128)(2,1)S(1)}, bf16[2,800,64]{1,2,0:T(8,128)(2,1)S(1)}, u32[]{:S(2)}, u32[]{:S(2)}) collective-permute-start(bf16[2,800,64]{1,2,0:T(8,128)(2,1)S(1)} %dynamic-slice_bitcast_fusion.11), channel_id=1, source_target_pairs={{0,8},{4,12},{8,0},{12,4},{16,24},{20,28},{24,16},{28,20},{1,9},{5... | collective-permute-start | bytes 614408 | tf_op jit(solution)/shard_map/ppermute | solution.py:96
  427.9 10.3 %collective-permute-start.42 = (bf16[64,800]{1,0:T(8,128)(2,1)S(1)}, bf16[64,800]{1,0:T(8,128)(2,1)S(1)}, u32[]{:S(2)}, u32[]{:S(2)}) collective-permute-start(bf16[64,800]{1,0:T(8,128)(2,1)S(1)} %dynamic-slice_bitcast_fusion.16), channel_id=1, source_target_pairs={{0,16},{4,20},{8,24},{12,28},{16,0},{20,4},{24,8},{28,12},{1,17},{... | collective-permute-start | bytes 307208 | tf_op jit(solution)/shard_map/ppermute | solution.py:96
  431.2 8.3 %collective-permute-start.47 = (bf16[800,64]{0,1:T(8,128)(2,1)S(1)}, bf16[800,64]{0,1:T(8,128)(2,1)S(1)}, u32[]{:S(2)}, u32[]{:S(2)}) collective-permute-start(bf16[800,64]{0,1:T(8,128)(2,1)S(1)} %dynamic-slice_bitcast_fusion.15), channel_id=1, source_target_pairs={{0,16},{4,20},{8,24},{12,28},{16,0},{20,4},{24,8},{28,12},{1,17},{... | collective-permute-start | bytes 307208 | tf_op jit(solution)/shard_map/ppermute | solution.py:96
  (90 other events, 366.6 us)
